TPU v7x, 128 devices: a whole 4x4x4 slice. The times are simulated.
128 devices in a mesh: pb: 4 (over y_lo, core), kv: 32 (over x, y_hi, z).
Axes of the slice: x: 4, y: 4 (y_hi: 2, y_lo: 2; y = y_hi * 2 + y_lo), z: 4, core: 2. Of those that a mesh axis runs over, the one named last changes fastest.
Arguments:
- queries: bfloat16 [32768, 128], P(('pb', 'kv')), may hold values from -15 to 15
- query_tangent: bfloat16 [32768, 128], P(('pb', 'kv')), may hold values from -2 to 2
- keys: bfloat16 [32768, 128], P(('pb', 'kv')), may hold values from -8 to 8
- values: bfloat16 [32768, 128], P(('pb', 'kv')), may hold values from -6 to 6
- key_tangent: bfloat16 [32768, 128], P(('pb', 'kv')), may hold values from -2 to 2
- value_tangent: bfloat16 [32768, 128], P(('pb', 'kv')), may hold values from -6 to 6
- block_list: int32 [256, 32, 8], P('pb', 'kv'), may hold values from 0 to 255, as said below
- block_count: int32 [256, 32], P('pb', 'kv'), may hold values from 1 to 8, as said below
Outputs:
- attended: bfloat16 [32768, 128], P(('pb', 'kv'))
- attended_tangent: bfloat16 [32768, 128], P(('pb', 'kv'))
Inputs may be any that keep to these rules, and one draw needn't show every extreme that they name: `block_list`: entries for one query block and slab j are distinct key blocks g whose index g // (256 // 128) leaves remainder j when divided by 32; entries past block_count are valid but unused. `block_count`: the value 8 is reached in every key slab.
All inputs are finite; a program needn't handle non-finite values.
Results may differ from a plain program's by a relative error of at most 0.01.
Values may be sent and summed in bfloat16 or wider, within the bound.
No kernel may reach another device: no remote copies, remote signals or barrier semaphores. Data moves between devices by JAX's collectives and lax.ppermute only.
A program may use at most 128 MiB of HBM per device.

v0:
```python
import math

import jax
import jax.numpy as jnp
import numpy as np
from jax import lax
from jax.experimental import pallas as pl
from jax.experimental.pallas import tpu as pltpu
from jax.sharding import Mesh
from jax.sharding import PartitionSpec as P

BLK = 128
HD = 128
LMAX = 8
TOK = 256
NX, NZ = 4, 4
GROUP = 4
SCALE = 1.0 / math.sqrt(HD)
LOG2E = math.log2(math.e)
FLOOR = -1.0e30
STAT = 16
PART = 2 * BLK + STAT


def split3(x):
    hi = x.astype(jnp.bfloat16).astype(jnp.float32)
    mid = (x - hi).astype(jnp.bfloat16).astype(jnp.float32)
    return [hi, mid, x - hi - mid]


def attend_kernel(me_ref, *refs):
    tables, refs = refs[:4], refs[4:]
    q_refs, refs = refs[:4], refs[4:]
    k_refs, refs = refs[:10], refs[10:]
    out_refs, refs = refs[:8], refs[8:]
    q_buf, k_buf, vt_buf, wq_ref, m_ref, sum_ref, slope_ref, acc_ref, q_sem, k_sem = refs
    my_yl, my_c, my_x, my_yh, my_z = (me_ref[i] for i in range(5))

    q_copies = [pltpu.make_async_copy(ref, q_buf.at[i], q_sem.at[i]) for i, ref in enumerate(q_refs)]
    for copy in q_copies:
        copy.start()
    places = []
    for dc in range(2):
        for dx, dyl, size in ((0, 0, 2), (1, 0, 2), (3, 0, 2), (2, 0, 1), (2, 1, 1)):
            places.append(((dx * 2 + dc) * 2 + dyl, size))
    k_copies = []
    for i, (ref, (at, size)) in enumerate(zip(k_refs, places)):
        rows = pl.ds(at * 4 * TOK, size * 4 * TOK)
        k_copies.append(pltpu.make_async_copy(ref, k_buf.at[rows, :], k_sem.at[i]))
        k_copies[-1].start()
    for copy, (at, size) in zip(k_copies, places):
        copy.wait()
        for shard in range(at, at + size):
            for half in range(2):
                for part in range(2):
                    rows = pl.ds(shard * 4 * TOK + (2 + part) * TOK + half * BLK, BLK)
                    vt_buf[shard * 2 + half, pl.ds(part * HD, HD), :] = k_buf[rows, :].T
    for copy in q_copies:
        copy.wait()
    for sub in range(2):
        wq_ref[sub, HD:, :HD] = jnp.zeros((HD, BLK), jnp.bfloat16)

    for place in range(8):
        dyh, dz = place // 4, place % 4
        row0 = my_x * 16 + (my_yh ^ dyh) * 8 + ((my_z - dz + NZ) & 3) * 2
        ends = []
        for sub in range(2):
            stops, stop = [], jnp.int32(0)
            for table in tables:
                stop = stop + table[row0 + sub, LMAX]
                stops.append(stop)
            ends.append(stops)
            at = dyh * 2 * TOK + sub * BLK
            qx = q_buf[dz, pl.ds(at, BLK), :].T
            wq_ref[sub, :HD, :HD] = qx
            wq_ref[sub, HD:, HD:] = qx
            wq_ref[sub, :HD, HD:] = q_buf[dz, pl.ds(at + TOK, BLK), :].T
        m_ref[...] = jnp.full_like(m_ref, FLOOR)
        sum_ref[...] = jnp.zeros_like(sum_ref)
        slope_ref[...] = jnp.zeros_like(slope_ref)
        acc_ref[...] = jnp.zeros_like(acc_ref)

        def pick(sub, at):
            stops = ends[sub]
            penalty = jnp.where(at < stops[-1], jnp.float32(0.0), jnp.float32(-FLOOR))
            at = jnp.minimum(at, stops[-1] - 1)
            row = row0 + sub
            g = tables[0][row, jnp.minimum(at, LMAX - 1)]
            for table, stop in zip(tables[1:], stops):
                g = jnp.where(at >= stop, table[row, jnp.clip(at - stop, 0, LMAX - 1)], g)
            shard = g >> 1
            x, c, yl = (shard >> 3) & 3, (shard >> 5) & 1, (shard >> 6) & 1
            shard = ((((my_x - x + NX) & 3) * 2 + (c ^ my_c)) * 2) + (yl ^ my_yl)
            return shard, g & 1, penalty

        def step(n, carry):
            for sub in range(2):
                picked = [pick(sub, n * GROUP + i) for i in range(GROUP)]
                keys = []
                for shard, half, _ in picked:
                    at = pl.multiple_of(shard * (4 * TOK) + half * BLK, BLK)
                    keys.append(
                        jnp.concatenate([k_buf[pl.ds(at, BLK), :], k_buf[pl.ds(at + TOK, BLK), :]], axis=1)
                    )
                dots = jnp.dot(
                    jnp.concatenate(keys, axis=0), wq_ref[sub], preferred_element_type=jnp.float32
                )
                s, st = dots[:, :BLK], dots[:, BLK:]
                top = jnp.max(s, axis=0, keepdims=True) * (SCALE * LOG2E)
                old = m_ref[sub, 0:1, :]
                new = jnp.maximum(old, top)
                alpha = jnp.exp2(old - new)
                total = sum_ref[sub, 0:1, :] * alpha
                slope = slope_ref[sub, 0:1, :] * alpha
                both = []
                for i, (_, _, penalty) in enumerate(picked):
                    rows = slice(i * BLK, (i + 1) * BLK)
                    w = jnp.exp2(s[rows] * (SCALE * LOG2E) - (new + penalty))
                    wt = w * st[rows]
                    total = total + jnp.sum(w, axis=0, keepdims=True)
                    slope = slope + jnp.sum(wt, axis=0, keepdims=True)
                    both.append(
                        jnp.concatenate([w.astype(jnp.bfloat16), wt.astype(jnp.bfloat16)], axis=1)
                    )
                values = jnp.concatenate([vt_buf[shard * 2 + half] for shard, half, _ in picked], axis=1)
                out = jnp.dot(values, jnp.concatenate(both, axis=0), preferred_element_type=jnp.float32)
                m_ref[sub, 0:1, :] = new
                sum_ref[sub, 0:1, :] = total
                slope_ref[sub, 0:1, :] = slope
                acc_ref[sub, :HD, :] = acc_ref[sub, :HD, :] * alpha + out[:HD, :BLK]
                acc_ref[sub, HD:, :] = (
                    acc_ref[sub, HD:, :] * alpha + out[:HD, BLK:] * SCALE + out[HD:, :BLK]
                )
            return carry

        steps = (jnp.maximum(ends[0][-1], ends[1][-1]) + GROUP - 1) // GROUP
        lax.fori_loop(0, steps, step, 0)

        out_ref = out_refs[place]
        for sub in range(2):
            total = sum_ref[sub, 0:1, :]
            inv = 1.0 / total
            slope = slope_ref[sub, 0:1, :] * (inv * SCALE)
            o = acc_ref[sub, :HD, :] * inv
            t = acc_ref[sub, HD:, :] * inv - slope * o
            rows = split3(m_ref[sub, 0:1, :]) + split3(total) + split3(slope)
            rows.append(jnp.zeros((STAT - 9, BLK), jnp.float32))
            base = sub * PART
            out_ref[pl.ds(base, HD), :] = o.astype(jnp.bfloat16)
            out_ref[pl.ds(base + HD, HD), :] = t.astype(jnp.bfloat16)
            out_ref[pl.ds(base + 2 * HD, STAT), :] = jnp.concatenate(rows, axis=0).astype(jnp.bfloat16)


def combine_kernel(*refs):
    part_refs, (o_ref, t_ref) = refs[:8], refs[8:]
    for sub in range(2):
        base = sub * PART
        peaks, totals, slopes = [], [], []
        for ref in part_refs:
            stats = ref[pl.ds(base + 2 * HD, STAT), :].astype(jnp.float32)
            for which, kept in enumerate((peaks, totals, slopes)):
                at = 3 * which
                kept.append(stats[at:at + 1] + stats[at + 1:at + 2] + stats[at + 2:at + 3])
        peak = peaks[0]
        for p in peaks[1:]:
            peak = jnp.maximum(peak, p)
        shares = [l * jnp.exp2(p - peak) for l, p in zip(totals, peaks)]
        inv = 1.0 / sum(shares[1:], shares[0])
        shares = [a * inv for a in shares]
        slope = sum((a * s for a, s in zip(shares[1:], slopes[1:])), shares[0] * slopes[0])
        o = jnp.zeros((HD, BLK), jnp.float32)
        t = jnp.zeros((HD, BLK), jnp.float32)
        for ref, a, s in zip(part_refs, shares, slopes):
            oj = ref[pl.ds(base, HD), :].astype(jnp.float32)
            tj = ref[pl.ds(base + HD, HD), :].astype(jnp.float32)
            o = o + a * oj
            t = t + a * tj + (a * (s - slope)) * oj
        o_ref[pl.ds(sub * BLK, BLK), :] = o.T.astype(jnp.bfloat16)
        t_ref[pl.ds(sub * BLK, BLK), :] = t.T.astype(jnp.bfloat16)


def shift(size, k):
    return [(i, (i + k) % size) for i in range(size)]


def attend(me, tables, queries, keys):
    smem = pl.BlockSpec(memory_space=pltpu.SMEM)
    vmem = pl.BlockSpec(memory_space=pltpu.VMEM)
    anywhere = pl.BlockSpec(memory_space=pl.ANY)
    return pl.pallas_call(
        attend_kernel,
        out_shape=[jax.ShapeDtypeStruct((2 * PART, BLK), jnp.bfloat16)] * 8,
        in_specs=[smem] * 5 + [anywhere] * 14,
        out_specs=[vmem] * 8,
        scratch_shapes=[
            pltpu.VMEM((4, 4 * TOK, HD), jnp.bfloat16),
            pltpu.VMEM((16 * 4 * TOK, HD), jnp.bfloat16),
            pltpu.VMEM((32, 2 * HD, BLK), jnp.bfloat16),
            pltpu.VMEM((2, 2 * HD, 2 * BLK), jnp.bfloat16),
            pltpu.VMEM((2, 8, BLK), jnp.float32),
            pltpu.VMEM((2, 8, BLK), jnp.float32),
            pltpu.VMEM((2, 8, BLK), jnp.float32),
            pltpu.VMEM((2, 2 * HD, BLK), jnp.float32),
            pltpu.SemaphoreType.DMA((4,)),
            pltpu.SemaphoreType.DMA((10,)),
        ],
        compiler_params=pltpu.CompilerParams(vmem_limit_bytes=40 * 2**20),
        name="attend",
    )(me, *tables, *queries, *keys)


def shards(q, qt, k, v, kt, vt, block_list, block_count):
    me = jnp.stack([lax.axis_index(a) for a in ("yl", "c", "x", "yh", "z")]).astype(jnp.int32)
    flip = [(0, 1), (1, 0)]
    shard = 4 * TOK

    own = jnp.concatenate([k, kt, v, vt], axis=0)
    pair = jnp.concatenate([own, lax.ppermute(own, "yl", flip)], axis=0)
    ahead = lax.ppermute(pair, "x", shift(NX, 1))
    behind = lax.ppermute(pair, "x", shift(NX, 3))
    far0 = lax.ppermute(ahead[:shard], "x", shift(NX, 1))
    far1 = lax.ppermute(behind[shard:], "x", shift(NX, 3))
    keys = [pair, ahead, behind, far0, far1]
    keys = keys + [lax.ppermute(a, "c", flip) for a in keys]

    asked = jnp.concatenate([q, qt], axis=0)
    asked = jnp.concatenate([asked, lax.ppermute(asked, "yh", flip)], axis=0)
    queries = [asked] + [lax.ppermute(asked, "z", shift(NZ, d)) for d in (1, 2, 3)]

    table = jnp.concatenate([block_list[:, 0, :], block_count], axis=1)
    tables = [table] + [lax.ppermute(table, "x", shift(NX, d)) for d in (1, 2, 3)]

    parts = attend(me, tables, queries, keys)

    back = [parts[0]]
    for place in range(1, 8):
        dyh, dz = place // 4, place % 4
        route = [
            ((yh ^ dyh) * NZ + (z + dz) % NZ, yh * NZ + z) for yh in range(2) for z in range(NZ)
        ]
        back.append(lax.ppermute(parts[place], ("yh", "z"), route))
    vmem = pl.BlockSpec(memory_space=pltpu.VMEM)
    return tuple(
        pl.pallas_call(
            combine_kernel,
            out_shape=[jax.ShapeDtypeStruct((TOK, HD), jnp.bfloat16)] * 2,
            in_specs=[vmem] * 8,
            out_specs=[vmem] * 2,
            compiler_params=pltpu.CompilerParams(vmem_limit_bytes=16 * 2**20),
            name="combine",
        )(*back)
    )


def solution(mesh):
    split = Mesh(np.asarray(mesh.devices).reshape(2, 2, NX, 2, NZ), ("yl", "c", "x", "yh", "z"))
    pb, kv = ("yl", "c"), ("x", "yh", "z")
    row = P(pb + kv, None)
    return jax.shard_map(
        shards,
        mesh=split,
        in_specs=(row,) * 6 + (P(pb, kv, None), P(pb, kv)),
        out_specs=(row, row),
        check_vma=False,
    )
```

profile of v0, /device:TPU:0, one launch (start us, length us, event | category | flops | bytes accessed | tf_op | source)
XLA Modules:
  0.0 111.5 jit_solution(15058277520464579260)
XLA Ops:
  2.1 2.9 %collective-permute-start.2 = (s32[64,9]{1,0:T(8,128)S(1)}, s32[64,9]{1,0:T(8,128)S(1)}, u32[]{:S(2)}, u32[]{:S(2)}) collective-permute-start(s32[64,9]{1,0:T(8,128)S(1)} %copy.15.refs_0_), channel_id=1, source_target_pairs={{0,24},{8,0},{16,8},{24,16},{1,25},{9,1},{17,9},{25,17},{2,26},{10... | collective-permute-start | bytes 6920 | tf_op jit(solution)/shard_map/ppermute | solution.py:231
  5.9 3.3 %collective-permute-start.3 = (bf16[512,128]{1,0:T(8,128)(2,1)S(1)}, bf16[512,128]{1,0:T(8,128)(2,1)S(1)}, u32[]{:S(2)}, u32[]{:S(2)}) collective-permute-start(bf16[512,128]{1,0:T(8,128)(2,1)S(1)} %pad_maximum_fusion.1), channel_id=1, source_target_pairs={{0,4},{4,0},{1,5},{5,1},{2,6},{6,2},{3,7},{7,3},{8,12},{12,8},{9,1... | collective-permute-start | bytes 393224 | tf_op jit(solution)/shard_map/ppermute | solution.py:227
  10.0 8.4 %collective-permute-done.7 = bf16[1024,128]{1,0:T(8,128)(2,1)S(1)} collective-permute-done((bf16[1024,128]{1,0:T(8,128)(2,1)S(1)}, bf16[1024,128]{1,0:T(8,128)(2,1)S(1)}, u32[]{:S(2)}, u32[]{:S(2)}) %collective-permute-start.7) | collective-permute-done | bytes 262176 | tf_op jit(solution)/shard_map/ppermute | solution.py:218
  19.4 1.2 %collective-permute-start.8 = (bf16[2048,128]{1,0:T(8,128)(2,1)S(1)}, bf16[2048,128]{1,0:T(8,128)(2,1)S(1)}, u32[]{:S(2)}, u32[]{:S(2)}) collective-permute-start(bf16[2048,128]{1,0:T(8,128)(2,1)S(1)} %constant_dynamic-update-slice_fusion.3.refs_8_), channel_id=1, source_target_pairs={{0,8},{8,16},{16,24},{24,0},{1,9},{9,17},{17,25},{25,1},{2,10},{10... | collective-permute-start | bytes 1572872 | tf_op jit(solution)/shard_map/ppermute | solution.py:219
  20.6 4.1 %collective-permute-start.6 = (bf16[1024,128]{1,0:T(8,128)(2,1)S(1)}, bf16[1024,128]{1,0:T(8,128)(2,1)S(1)}, u32[]{:S(2)}, u32[]{:S(2)}) collective-permute-start(bf16[1024,128]{1,0:T(8,128)(2,1)S(1)} %constant_dynamic-update-slice_fusion.refs_4_), channel_id=1, source_target_pairs={{0,3},{1,0},{2,1},{3,2},{4,7},{5,4},{6,5},{7,6},{8,11},{9,8},{10,9... | collective-permute-start | bytes 786440 | tf_op jit(solution)/shard_map/ppermute | solution.py:228
  24.7 1.3 %collective-permute-start.4 = (bf16[1024,128]{1,0:T(8,128)(2,1)S(1)}, bf16[1024,128]{1,0:T(8,128)(2,1)S(1)}, u32[]{:S(2)}, u32[]{:S(2)}) collective-permute-start(bf16[1024,128]{1,0:T(8,128)(2,1)S(1)} %constant_dynamic-update-slice_fusion.refs_4_), channel_id=1, source_target_pairs={{0,1},{1,2},{2,3},{3,0},{4,5},{5,6},{6,7},{7,4},{8,9},{9,10},{10,1... | collective-permute-start | bytes 786440 | tf_op jit(solution)/shard_map/ppermute | solution.py:228
  26.0 5.0 %collective-permute-done.9.refs_10_ = bf16[2048,128]{1,0:T(8,128)(2,1)S(1)} collective-permute-done((bf16[2048,128]{1,0:T(8,128)(2,1)S(1)}, bf16[2048,128]{1,0:T(8,128)(2,1)S(1)}, u32[]{:S(2)}, u32[]{:S(2)}) %collective-permute-start.9) | collective-permute-done | bytes 524320 | tf_op jit(solution)/shard_map/ppermute | solution.py:220
  32.8 1.1 %collective-permute-start = (s32[64,9]{1,0:T(8,128)S(1)}, s32[64,9]{1,0:T(8,128)S(1)}, u32[]{:S(2)}, u32[]{:S(2)}) collective-permute-start(s32[64,9]{1,0:T(8,128)S(1)} %copy.15.refs_0_), channel_id=1, source_target_pairs={{0,8},{8,16},{16,24},{24,0},{1,9},{9,17},{17,25},{25,1},{2,10},{10... | collective-permute-start | bytes 6920 | tf_op jit(solution)/shard_map/ppermute | solution.py:231
  33.9 2.5 %collective-permute-done.1.refs_2_ = s32[64,9]{1,0:T(8,128)S(1)} collective-permute-done((s32[64,9]{1,0:T(8,128)S(1)}, s32[64,9]{1,0:T(8,128)S(1)}, u32[]{:S(2)}, u32[]{:S(2)}) %collective-permute-start.1) | collective-permute-done | bytes 2336 | tf_op jit(solution)/shard_map/ppermute | solution.py:231
  36.4 1.5 %collective-permute-done.refs_1_ = s32[64,9]{1,0:T(8,128)S(1)} collective-permute-done((s32[64,9]{1,0:T(8,128)S(1)}, s32[64,9]{1,0:T(8,128)S(1)}, u32[]{:S(2)}, u32[]{:S(2)}) %collective-permute-start) | collective-permute-done | bytes 2336 | tf_op jit(solution)/shard_map/ppermute | solution.py:231
  39.2 1.4 %collective-permute-start.10 = (bf16[1024,128]{1,0:T(8,128)(2,1)S(1)}, bf16[1024,128]{1,0:T(8,128)(2,1)}, u32[]{:S(2)}, u32[]{:S(2)}) collective-permute-start(bf16[1024,128]{1,0:T(8,128)(2,1)S(1)} %slice.8), channel_id=1, source_target_pairs={{0,8},{8,16},{16,24},{24,0},{1,9},{9,17},{17,25},{25,1},{2,10},{10... | collective-permute-start | bytes 786440 | tf_op jit(solution)/shard_map/ppermute | solution.py:221
  42.5 2.7 %collective-permute-done.11.refs_12_ = bf16[1024,128]{1,0:T(8,128)(2,1)} collective-permute-done((bf16[1024,128]{1,0:T(8,128)(2,1)S(1)}, bf16[1024,128]{1,0:T(8,128)(2,1)}, u32[]{:S(2)}, u32[]{:S(2)}) %collective-permute-start.11) | collective-permute-done | bytes 262176 | tf_op jit(solution)/shard_map/ppermute | solution.py:222
  45.3 3.7 %collective-permute-done.10.refs_11_ = bf16[1024,128]{1,0:T(8,128)(2,1)} collective-permute-done((bf16[1024,128]{1,0:T(8,128)(2,1)S(1)}, bf16[1024,128]{1,0:T(8,128)(2,1)}, u32[]{:S(2)}, u32[]{:S(2)}) %collective-permute-start.10) | collective-permute-done | bytes 262176 | tf_op jit(solution)/shard_map/ppermute | solution.py:221
  49.0 1.8 %collective-permute-done.15.refs_16_ = bf16[1024,128]{1,0:T(8,128)(2,1)} collective-permute-done((bf16[1024,128]{1,0:T(8,128)(2,1)}, bf16[1024,128]{1,0:T(8,128)(2,1)}, u32[]{:S(2)}, u32[]{:S(2)}) %collective-permute-start.15) | collective-permute-done | bytes 262176 | tf_op jit(solution)/shard_map/ppermute | solution.py:224
  53.7 26.5 %attend.1 = (bf16[544,128]{1,0:T(8,128)(2,1)S(1)}, bf16[544,128]{1,0:T(8,128)(2,1)S(1)}, bf16[544,128]{1,0:T(8,128)(2,1)S(1)}, bf16[544,128]{1,0:T(8,128)(2,1)S(...) custom-call(s32[5]{0:T(128)S(1)} %stack.23.me_ref, ...), custom_call_target="tpu_custom_call" | custom-call | tf_op jit(solution)/shard_map/attend/pallas_call | solution.py:190
  80.2 4.9 %collective-permute-start.17 = (bf16[544,128]{1,0:T(8,128)(2,1)S(1)}, bf16[544,128]{1,0:T(8,128)(2,1)S(1)}, u32[]{:S(2)}, u32[]{:S(2)}) collective-permute-start(bf16[544,128]{1,0:T(8,128)(2,1)S(1)} %get-tuple-element.11), channel_id=1, source_target_pairs={{1,0},{2,1},{3,2},{0,3},{5,4},{6,5},{7,6},{4,7},{9,8},{10,9},{11,1... | collective-permute-start | bytes 417800 | tf_op jit(solution)/shard_map/ppermute | solution.py:241
  85.0 5.9 %collective-permute-start.18 = (bf16[544,128]{1,0:T(8,128)(2,1)S(1)}, bf16[544,128]{1,0:T(8,128)(2,1)S(1)}, u32[]{:S(2)}, u32[]{:S(2)}) collective-permute-start(bf16[544,128]{1,0:T(8,128)(2,1)S(1)} %get-tuple-element.12), channel_id=1, source_target_pairs={{2,0},{3,1},{0,2},{1,3},{6,4},{7,5},{4,6},{5,7},{10,8},{11,9},{8,1... | collective-permute-start | bytes 417800 | tf_op jit(solution)/shard_map/ppermute | solution.py:241
  90.9 1.7 %collective-permute-start.20 = (bf16[544,128]{1,0:T(8,128)(2,1)S(1)}, bf16[544,128]{1,0:T(8,128)(2,1)S(1)}, u32[]{:S(2)}, u32[]{:S(2)}) collective-permute-start(bf16[544,128]{1,0:T(8,128)(2,1)S(1)} %get-tuple-element.14), channel_id=1, source_target_pairs={{4,0},{5,1},{6,2},{7,3},{0,4},{1,5},{2,6},{3,7},{12,8},{13,9},{14,... | collective-permute-start | bytes 417800 | tf_op jit(solution)/shard_map/ppermute | solution.py:241
  92.6 4.5 %collective-permute-start.21 = (bf16[544,128]{1,0:T(8,128)(2,1)S(1)}, bf16[544,128]{1,0:T(8,128)(2,1)S(1)}, u32[]{:S(2)}, u32[]{:S(2)}) collective-permute-start(bf16[544,128]{1,0:T(8,128)(2,1)S(1)} %get-tuple-element.15), channel_id=1, source_target_pairs={{5,0},{6,1},{7,2},{4,3},{1,4},{2,5},{3,6},{0,7},{13,8},{14,9},{15,... | collective-permute-start | bytes 417800 | tf_op jit(solution)/shard_map/ppermute | solution.py:241
  97.1 2.7 %collective-permute-start.23 = (bf16[544,128]{1,0:T(8,128)(2,1)S(1)}, bf16[544,128]{1,0:T(8,128)(2,1)S(1)}, u32[]{:S(2)}, u32[]{:S(2)}) collective-permute-start(bf16[544,128]{1,0:T(8,128)(2,1)S(1)} %get-tuple-element.17), channel_id=1, source_target_pairs={{7,0},{4,1},{5,2},{6,3},{3,4},{0,5},{1,6},{2,7},{15,8},{12,9},{13,... | collective-permute-start | bytes 417800 | tf_op jit(solution)/shard_map/ppermute | solution.py:241
  99.9 1.4 %collective-permute-done.21.refs_5_ = bf16[544,128]{1,0:T(8,128)(2,1)S(1)} collective-permute-done((bf16[544,128]{1,0:T(8,128)(2,1)S(1)}, bf16[544,128]{1,0:T(8,128)(2,1)S(1)}, u32[]{:S(2)}, u32[]{:S(2)}) %collective-permute-start.21) | collective-permute-done | bytes 139296 | tf_op jit(solution)/shard_map/ppermute | solution.py:241
  101.3 6.2 %collective-permute-done.22.refs_6_ = bf16[544,128]{1,0:T(8,128)(2,1)S(1)} collective-permute-done((bf16[544,128]{1,0:T(8,128)(2,1)S(1)}, bf16[544,128]{1,0:T(8,128)(2,1)S(1)}, u32[]{:S(2)}, u32[]{:S(2)}) %collective-permute-start.22) | collective-permute-done | bytes 139296 | tf_op jit(solution)/shard_map/ppermute | solution.py:241
  107.5 2.9 %collective-permute-done.23.refs_7_ = bf16[544,128]{1,0:T(8,128)(2,1)S(1)} collective-permute-done((bf16[544,128]{1,0:T(8,128)(2,1)S(1)}, bf16[544,128]{1,0:T(8,128)(2,1)S(1)}, u32[]{:S(2)}, u32[]{:S(2)}) %collective-permute-start.23) | collective-permute-done | bytes 139296 | tf_op jit(solution)/shard_map/ppermute | solution.py:241
  110.5 1.1 combine.1
  (67 shorter events, 12.1 us)
Async XLA Ops:
  2.1 22.6 %collective-permute-start.2 = (s32[64,9]{1,0:T(8,128)S(1)}, s32[64,9]{1,0:T(8,128)S(1)}, u32[]{:S(2)}, u32[]{:S(2)}) collective-permute-start(s32[64,9]{1,0:T(8,128)S(1)} %copy.15.refs_0_), channel_id=1, source_target_pairs={{0,24},{8,0},{16,8},{24,16},{1,25},{9,1},{17,9},{25,17},{2,26},{10... | collective-permute-start | bytes 6920 | tf_op jit(solution)/shard_map/ppermute | solution.py:231
  5.9 14.7 %collective-permute-start.3 = (bf16[512,128]{1,0:T(8,128)(2,1)S(1)}, bf16[512,128]{1,0:T(8,128)(2,1)S(1)}, u32[]{:S(2)}, u32[]{:S(2)}) collective-permute-start(bf16[512,128]{1,0:T(8,128)(2,1)S(1)} %pad_maximum_fusion.1), channel_id=1, source_target_pairs={{0,4},{4,0},{1,5},{5,1},{2,6},{6,2},{3,7},{7,3},{8,12},{12,8},{9,1... | collective-permute-start | bytes 393224 | tf_op jit(solution)/shard_map/ppermute | solution.py:227
  9.2 9.2 %collective-permute-start.7 = (bf16[1024,128]{1,0:T(8,128)(2,1)S(1)}, bf16[1024,128]{1,0:T(8,128)(2,1)S(1)}, u32[]{:S(2)}, u32[]{:S(2)}) collective-permute-start(bf16[1024,128]{1,0:T(8,128)(2,1)S(1)} %pad_maximum_fusion), channel_id=1, source_target_pairs={{0,64},{64,0},{1,65},{65,1},{2,66},{66,2},{3,67},{67,3},{4,68},{68... | collective-permute-start | bytes 786440 | tf_op jit(solution)/shard_map/ppermute | solution.py:218
  18.5 12.5 %collective-permute-start.9 = (bf16[2048,128]{1,0:T(8,128)(2,1)S(1)}, bf16[2048,128]{1,0:T(8,128)(2,1)S(1)}, u32[]{:S(2)}, u32[]{:S(2)}) collective-permute-start(bf16[2048,128]{1,0:T(8,128)(2,1)S(1)} %constant_dynamic-update-slice_fusion.3.refs_8_), channel_id=1, source_target_pairs={{0,24},{8,0},{16,8},{24,16},{1,25},{9,1},{17,9},{25,17},{2,26},{10... | collective-permute-start | bytes 1572872 | tf_op jit(solution)/shard_map/ppermute | solution.py:220
  19.4 13.4 %collective-permute-start.8 = (bf16[2048,128]{1,0:T(8,128)(2,1)S(1)}, bf16[2048,128]{1,0:T(8,128)(2,1)S(1)}, u32[]{:S(2)}, u32[]{:S(2)}) collective-permute-start(bf16[2048,128]{1,0:T(8,128)(2,1)S(1)} %constant_dynamic-update-slice_fusion.3.refs_8_), channel_id=1, source_target_pairs={{0,8},{8,16},{16,24},{24,0},{1,9},{9,17},{17,25},{25,1},{2,10},{10... | collective-permute-start | bytes 1572872 | tf_op jit(solution)/shard_map/ppermute | solution.py:219
  20.6 17.8 %collective-permute-start.6 = (bf16[1024,128]{1,0:T(8,128)(2,1)S(1)}, bf16[1024,128]{1,0:T(8,128)(2,1)S(1)}, u32[]{:S(2)}, u32[]{:S(2)}) collective-permute-start(bf16[1024,128]{1,0:T(8,128)(2,1)S(1)} %constant_dynamic-update-slice_fusion.refs_4_), channel_id=1, source_target_pairs={{0,3},{1,0},{2,1},{3,2},{4,7},{5,4},{6,5},{7,6},{8,11},{9,8},{10,9... | collective-permute-start | bytes 786440 | tf_op jit(solution)/shard_map/ppermute | solution.py:228
  24.7 15.9 %collective-permute-start.5 = (bf16[1024,128]{1,0:T(8,128)(2,1)S(1)}, bf16[1024,128]{1,0:T(8,128)(2,1)S(1)}, u32[]{:S(2)}, u32[]{:S(2)}) collective-permute-start(bf16[1024,128]{1,0:T(8,128)(2,1)S(1)} %constant_dynamic-update-slice_fusion.refs_4_), channel_id=1, source_target_pairs={{0,2},{1,3},{2,0},{3,1},{4,6},{5,7},{6,4},{7,5},{8,10},{9,11},{10,... | collective-permute-start | bytes 786440 | tf_op jit(solution)/shard_map/ppermute | solution.py:228
  24.7 16.6 %collective-permute-start.4 = (bf16[1024,128]{1,0:T(8,128)(2,1)S(1)}, bf16[1024,128]{1,0:T(8,128)(2,1)S(1)}, u32[]{:S(2)}, u32[]{:S(2)}) collective-permute-start(bf16[1024,128]{1,0:T(8,128)(2,1)S(1)} %constant_dynamic-update-slice_fusion.refs_4_), channel_id=1, source_target_pairs={{0,1},{1,2},{2,3},{3,0},{4,5},{5,6},{6,7},{7,4},{8,9},{9,10},{10,1... | collective-permute-start | bytes 786440 | tf_op jit(solution)/shard_map/ppermute | solution.py:228
  31.0 5.4 %collective-permute-start.1 = (s32[64,9]{1,0:T(8,128)S(1)}, s32[64,9]{1,0:T(8,128)S(1)}, u32[]{:S(2)}, u32[]{:S(2)}) collective-permute-start(s32[64,9]{1,0:T(8,128)S(1)} %copy.15.refs_0_), channel_id=1, source_target_pairs={{0,16},{8,24},{16,0},{24,8},{1,17},{9,25},{17,1},{25,9},{2,18},{10... | collective-permute-start | bytes 6920 | tf_op jit(solution)/shard_map/ppermute | solution.py:231
  32.8 5.1 %collective-permute-start = (s32[64,9]{1,0:T(8,128)S(1)}, s32[64,9]{1,0:T(8,128)S(1)}, u32[]{:S(2)}, u32[]{:S(2)}) collective-permute-start(s32[64,9]{1,0:T(8,128)S(1)} %copy.15.refs_0_), channel_id=1, source_target_pairs={{0,8},{8,16},{16,24},{24,0},{1,9},{9,17},{17,25},{25,1},{2,10},{10... | collective-permute-start | bytes 6920 | tf_op jit(solution)/shard_map/ppermute | solution.py:231
  36.4 12.6 %collective-permute-start.12 = (bf16[2048,128]{1,0:T(8,128)(2,1)S(1)}, bf16[2048,128]{1,0:T(8,128)(2,1)S(1)}, u32[]{:S(2)}, u32[]{:S(2)}) collective-permute-start(bf16[2048,128]{1,0:T(8,128)(2,1)S(1)} %constant_dynamic-update-slice_fusion.3.refs_8_), channel_id=1, source_target_pairs={{0,32},{32,0},{1,33},{33,1},{2,34},{34,2},{3,35},{35,3},{4,36},{36... | collective-permute-start | bytes 1572872 | tf_op jit(solution)/shard_map/ppermute | solution.py:224
  37.9 7.4 %collective-permute-start.11 = (bf16[1024,128]{1,0:T(8,128)(2,1)S(1)}, bf16[1024,128]{1,0:T(8,128)(2,1)}, u32[]{:S(2)}, u32[]{:S(2)}) collective-permute-start(bf16[1024,128]{1,0:T(8,128)(2,1)S(1)} %slice.9), channel_id=1, source_target_pairs={{0,24},{8,0},{16,8},{24,16},{1,25},{9,1},{17,9},{25,17},{2,26},{10... | collective-permute-start | bytes 786440 | tf_op jit(solution)/shard_map/ppermute | solution.py:222
  39.2 9.8 %collective-permute-start.10 = (bf16[1024,128]{1,0:T(8,128)(2,1)S(1)}, bf16[1024,128]{1,0:T(8,128)(2,1)}, u32[]{:S(2)}, u32[]{:S(2)}) collective-permute-start(bf16[1024,128]{1,0:T(8,128)(2,1)S(1)} %slice.8), channel_id=1, source_target_pairs={{0,8},{8,16},{16,24},{24,0},{1,9},{9,17},{17,25},{25,1},{2,10},{10... | collective-permute-start | bytes 786440 | tf_op jit(solution)/shard_map/ppermute | solution.py:221
  41.3 7.7 %collective-permute-start.14 = (bf16[2048,128]{1,0:T(8,128)(2,1)S(1)}, bf16[2048,128]{1,0:T(8,128)(2,1)S(1)}, u32[]{:S(2)}, u32[]{:S(2)}) collective-permute-start(bf16[2048,128]{1,0:T(8,128)(2,1)S(1)} %collective-permute-done.9.refs_10_), channel_id=1, source_target_pairs={{0,32},{32,0},{1,33},{33,1},{2,34},{34,2},{3,35},{35,3},{4,36},{36... | collective-permute-start | bytes 1572872 | tf_op jit(solution)/shard_map/ppermute | solution.py:224
  42.0 8.8 %collective-permute-start.13 = (bf16[2048,128]{1,0:T(8,128)(2,1)S(1)}, bf16[2048,128]{1,0:T(8,128)(2,1)S(1)}, u32[]{:S(2)}, u32[]{:S(2)}) collective-permute-start(bf16[2048,128]{1,0:T(8,128)(2,1)S(1)} %collective-permute-done.8.refs_9_), channel_id=1, source_target_pairs={{0,32},{32,0},{1,33},{33,1},{2,34},{34,2},{3,35},{35,3},{4,36},{36... | collective-permute-start | bytes 1572872 | tf_op jit(solution)/shard_map/ppermute | solution.py:224
  45.2 3.8 %collective-permute-start.16 = (bf16[1024,128]{1,0:T(8,128)(2,1)}, bf16[1024,128]{1,0:T(8,128)(2,1)}, u32[]{:S(2)}, u32[]{:S(2)}) collective-permute-start(bf16[1024,128]{1,0:T(8,128)(2,1)} %collective-permute-done.11.refs_12_), channel_id=1, source_target_pairs={{0,32},{32,0},{1,33},{33,1},{2,34},{34,2},{3,35},{35,3},{4,36},{36... | collective-permute-start | bytes 786440 | tf_op jit(solution)/shard_map/ppermute | solution.py:224
  48.9 1.9 %collective-permute-start.15 = (bf16[1024,128]{1,0:T(8,128)(2,1)}, bf16[1024,128]{1,0:T(8,128)(2,1)}, u32[]{:S(2)}, u32[]{:S(2)}) collective-permute-start(bf16[1024,128]{1,0:T(8,128)(2,1)} %collective-permute-done.10.refs_11_), channel_id=1, source_target_pairs={{0,32},{32,0},{1,33},{33,1},{2,34},{34,2},{3,35},{35,3},{4,36},{36... | collective-permute-start | bytes 786440 | tf_op jit(solution)/shard_map/ppermute | solution.py:224
  80.2 17.0 %collective-permute-start.17 = (bf16[544,128]{1,0:T(8,128)(2,1)S(1)}, bf16[544,128]{1,0:T(8,128)(2,1)S(1)}, u32[]{:S(2)}, u32[]{:S(2)}) collective-permute-start(bf16[544,128]{1,0:T(8,128)(2,1)S(1)} %get-tuple-element.11), channel_id=1, source_target_pairs={{1,0},{2,1},{3,2},{0,3},{5,4},{6,5},{7,6},{4,7},{9,8},{10,9},{11,1... | collective-permute-start | bytes 417800 | tf_op jit(solution)/shard_map/ppermute | solution.py:241
  85.0 12.1 %collective-permute-start.18 = (bf16[544,128]{1,0:T(8,128)(2,1)S(1)}, bf16[544,128]{1,0:T(8,128)(2,1)S(1)}, u32[]{:S(2)}, u32[]{:S(2)}) collective-permute-start(bf16[544,128]{1,0:T(8,128)(2,1)S(1)} %get-tuple-element.12), channel_id=1, source_target_pairs={{2,0},{3,1},{0,2},{1,3},{6,4},{7,5},{4,6},{5,7},{10,8},{11,9},{8,1... | collective-permute-start | bytes 417800 | tf_op jit(solution)/shard_map/ppermute | solution.py:241
  90.9 9.0 %collective-permute-start.19 = (bf16[544,128]{1,0:T(8,128)(2,1)S(1)}, bf16[544,128]{1,0:T(8,128)(2,1)S(1)}, u32[]{:S(2)}, u32[]{:S(2)}) collective-permute-start(bf16[544,128]{1,0:T(8,128)(2,1)S(1)} %get-tuple-element.13), channel_id=1, source_target_pairs={{3,0},{0,1},{1,2},{2,3},{7,4},{4,5},{5,6},{6,7},{11,8},{8,9},{9,10... | collective-permute-start | bytes 417800 | tf_op jit(solution)/shard_map/ppermute | solution.py:241
  90.9 9.0 %collective-permute-start.20 = (bf16[544,128]{1,0:T(8,128)(2,1)S(1)}, bf16[544,128]{1,0:T(8,128)(2,1)S(1)}, u32[]{:S(2)}, u32[]{:S(2)}) collective-permute-start(bf16[544,128]{1,0:T(8,128)(2,1)S(1)} %get-tuple-element.14), channel_id=1, source_target_pairs={{4,0},{5,1},{6,2},{7,3},{0,4},{1,5},{2,6},{3,7},{12,8},{13,9},{14,... | collective-permute-start | bytes 417800 | tf_op jit(solution)/shard_map/ppermute | solution.py:241
  92.6 8.7 %collective-permute-start.21 = (bf16[544,128]{1,0:T(8,128)(2,1)S(1)}, bf16[544,128]{1,0:T(8,128)(2,1)S(1)}, u32[]{:S(2)}, u32[]{:S(2)}) collective-permute-start(bf16[544,128]{1,0:T(8,128)(2,1)S(1)} %get-tuple-element.15), channel_id=1, source_target_pairs={{5,0},{6,1},{7,2},{4,3},{1,4},{2,5},{3,6},{0,7},{13,8},{14,9},{15,... | collective-permute-start | bytes 417800 | tf_op jit(solution)/shard_map/ppermute | solution.py:241
  97.1 10.4 %collective-permute-start.22 = (bf16[544,128]{1,0:T(8,128)(2,1)S(1)}, bf16[544,128]{1,0:T(8,128)(2,1)S(1)}, u32[]{:S(2)}, u32[]{:S(2)}) collective-permute-start(bf16[544,128]{1,0:T(8,128)(2,1)S(1)} %get-tuple-element.16), channel_id=1, source_target_pairs={{6,0},{7,1},{4,2},{5,3},{2,4},{3,5},{0,6},{1,7},{14,8},{15,9},{12,... | collective-permute-start | bytes 417800 | tf_op jit(solution)/shard_map/ppermute | solution.py:241
  97.1 13.3 %collective-permute-start.23 = (bf16[544,128]{1,0:T(8,128)(2,1)S(1)}, bf16[544,128]{1,0:T(8,128)(2,1)S(1)}, u32[]{:S(2)}, u32[]{:S(2)}) collective-permute-start(bf16[544,128]{1,0:T(8,128)(2,1)S(1)} %get-tuple-element.17), channel_id=1, source_target_pairs={{7,0},{4,1},{5,2},{6,3},{3,4},{0,5},{1,6},{2,7},{15,8},{12,9},{13,... | collective-permute-start | bytes 417800 | tf_op jit(solution)/shard_map/ppermute | solution.py:241
  (13 other events, 46.6 us)
where the time goes:
time: 112 us
  starting transfers between devices  38.6 us (34%)
  waiting for transfers between devices  37 us (33%)
  Pallas kernels  27.6 us (25%)
  local copies, waits for them, and re-layouts  5.96 us (5%)
  other arithmetic  1.59 us (1%)
    pallas_call x1, Pallas kernels, attend(): pl.pallas_call(attend_kernel, out_shape=[jax.ShapeDtypeStruct((2 * PART,...  26.5 us
    ppermute x7, starting transfers between devices, shards(): back.append(lax.ppermute(parts[place], ('yh', 'z'), route))  19.7 us
    ppermute x7, waiting for transfers between devices, shards(): back.append(lax.ppermute(parts[place], ('yh', 'z'), route))  10.6 us
    ppermute x1, waiting for transfers between devices, shards(): pair = jnp.concatenate([own, lax.ppermute(own, 'yl', flip)], axis=0)  8.36 us
    unnamed x32, local copies, waits for them, and re-layouts  5.69 us
    ppermute x3, starting transfers between devices, shards(): lax.ppermute(asked, 'z', shift(NZ, d))  5.37 us
    ppermute x1, waiting for transfers between devices, shards(): behind = lax.ppermute(pair, 'x', shift(NX, 3))  5 us
    ppermute x3, starting transfers between devices, shards(): lax.ppermute(table, 'x', shift(NX, d))  4.85 us
  transfers between devices with their start and end apart: 24, of which 11 were waited for; matrix products, arithmetic and copies ran while one was open for 1% of the time, Pallas kernels for 0%

commit v1 on v0

v1 whole, which is shorter than its diff:
```python
import functools
import math

import jax
import jax.numpy as jnp
import numpy as np
from jax import lax
from jax.experimental import pallas as pl
from jax.experimental.pallas import tpu as pltpu
from jax.sharding import Mesh
from jax.sharding import PartitionSpec as P

BLK = 128
HD = 128
LMAX = 8
TOK = 256
NX, NZ = 4, 4
GROUP = 4
SCALE = 1.0 / math.sqrt(HD)
LOG2E = math.log2(math.e)
FLOOR = -1.0e30
STAT = 16
PART = 2 * BLK + STAT
PIECES = ((1, 0, 2), (3, 0, 2), (2, 0, 1), (2, 1, 1))


def split3(x):
    hi = x.astype(jnp.bfloat16).astype(jnp.float32)
    mid = (x - hi).astype(jnp.bfloat16).astype(jnp.float32)
    return [hi, mid, x - hi - mid]


class Job:
    def __init__(self, name, slabs, places, pieces, fresh, final, keep, group, room):
        self.name, self.slabs, self.places, self.pieces = name, slabs, places, pieces
        self.fresh, self.final, self.keep, self.group, self.room = fresh, final, keep, group, room


def attend_kernel(job, me_ref, *refs):
    refs = list(refs)

    def take(n):
        out = refs[:n]
        del refs[:n]
        return out

    group, count = job.group, len(job.slabs)
    tables_in = take(count)
    if job.fresh:
        q_refs = take(4)
    else:
        wq_in, state_in = take(2)
    if job.pieces:
        k_refs = take(len(job.pieces))
    else:
        k_buf, vt_buf = take(2)
    if job.fresh:
        wq_out, state_out = take(2)
    else:
        out_refs = take(len(job.places))
    if job.keep:
        k_buf, vt_buf = take(2)
    tables, s_ref, top_ref, m_ref, sum_ref, slope_ref, acc_ref, t_sem = take(8)
    if job.fresh:
        q_buf, q_sem = take(2)
    if job.pieces:
        raw, k_sem = take(2)
        if not job.keep:
            k_buf, vt_buf = take(2)
    my_yl, my_c, my_x, my_yh, my_z = (me_ref[i] for i in range(5))
    first_row = pl.multiple_of(my_x * 16, 16)

    t_copies = [
        pltpu.make_async_copy(ref.at[pl.ds(first_row, 16), :], tables.at[i], t_sem.at[i])
        for i, ref in enumerate(tables_in)
    ]
    for copy in t_copies:
        copy.start()
    if job.fresh:
        q_copies = [pltpu.make_async_copy(ref, q_buf.at[i], q_sem.at[i]) for i, ref in enumerate(q_refs)]
        for copy in q_copies:
            copy.start()
    if job.pieces:
        k_copies = []
        for i, (ref, (at, size)) in enumerate(zip(k_refs, job.pieces)):
            rows = pl.ds(at * 4 * TOK, size * 4 * TOK)
            k_copies.append(pltpu.make_async_copy(ref, raw.at[rows, :], k_sem.at[i]))
            k_copies[-1].start()
        for copy, (at, size) in zip(k_copies, job.pieces):
            copy.wait()
            for shard in range(at, at + size):
                for half in range(2):
                    slot = shard * 2 + half
                    for part in range(2):
                        rows = pl.ds(shard * 4 * TOK + part * TOK + half * BLK, BLK)
                        k_buf[pl.ds(slot * BLK, BLK), pl.ds(part * HD, HD)] = raw[rows, :]
                        rows = pl.ds(shard * 4 * TOK + (2 + part) * TOK + half * BLK, BLK)
                        vt_buf[slot, pl.ds(part * HD, HD), :] = raw[rows, :].T
    if job.fresh:
        for copy in q_copies:
            copy.wait()
    for copy in t_copies:
        copy.wait()
    base_dx = min(job.slabs)

    for nth, place in enumerate(job.places):
        dyh, dz = place // 4, place % 4
        row0 = (my_yh ^ dyh) * 8 + ((my_z - dz + NZ) & 3) * 2
        ends = []
        for sub in range(2):
            stops, stop = [], jnp.int32(0)
            for i in range(count):
                stop = stop + tables[i, row0 + sub, LMAX]
                stops.append(stop)
            ends.append(stops)
            if job.fresh:
                at = dyh * 2 * TOK + sub * BLK
                qx = q_buf[dz, pl.ds(at, BLK), :].T
                wq_out[place * 2 + sub, HD:, :HD] = jnp.zeros((HD, BLK), jnp.bfloat16)
                wq_out[place * 2 + sub, :HD, :HD] = qx
                wq_out[place * 2 + sub, HD:, HD:] = qx
                wq_out[place * 2 + sub, :HD, HD:] = q_buf[dz, pl.ds(at + TOK, BLK), :].T
        wq = wq_out if job.fresh else wq_in
        if job.fresh:
            m_ref[...] = jnp.full_like(m_ref, FLOOR)
            sum_ref[...] = jnp.zeros_like(sum_ref)
            slope_ref[...] = jnp.zeros_like(slope_ref)
            acc_ref[...] = jnp.zeros_like(acc_ref)
        else:
            for sub in range(2):
                m_ref[sub] = state_in[place * 2 + sub, 0:8, :]
                sum_ref[sub] = state_in[place * 2 + sub, 8:16, :]
                slope_ref[sub] = state_in[place * 2 + sub, 16:24, :]
                acc_ref[sub] = state_in[place * 2 + sub, 24:280, :]

        def pick(sub, at, ends=ends, row0=row0):
            stops = ends[sub]
            penalty = jnp.where(at < stops[-1], jnp.float32(0.0), jnp.float32(-FLOOR))
            at = jnp.minimum(at, stops[-1] - 1)
            row = row0 + sub
            g = tables[0, row, jnp.minimum(at, LMAX - 1)]
            for i, stop in enumerate(stops[:-1]):
                g = jnp.where(at >= stop, tables[i + 1, row, jnp.clip(at - stop, 0, LMAX - 1)], g)
            shard = g >> 1
            x, c, yl = (shard >> 3) & 3, (shard >> 5) & 1, (shard >> 6) & 1
            dx = (my_x - x + NX) & 3
            slot = ((((dx - base_dx) * 2 + (c ^ my_c)) * 2) + (yl ^ my_yl)) * 2 + (g & 1)
            return slot, penalty

        def score(sub, n, pick=pick, place=place):
            keys = []
            for i in range(group):
                slot, _ = pick(sub, n * group + i)
                keys.append(k_buf[pl.ds(pl.multiple_of(slot * BLK, BLK), BLK), :])
            dots = jnp.dot(
                jnp.concatenate(keys, axis=0), wq[place * 2 + sub], preferred_element_type=jnp.float32
            )
            s_ref[sub] = dots
            top_ref[sub, 0:1, :] = jnp.max(dots[:, :BLK], axis=0, keepdims=True) * (SCALE * LOG2E)

        def absorb(sub, n, pick=pick):
            picked = [pick(sub, n * group + i) for i in range(group)]
            old = m_ref[sub, 0:1, :]
            new = jnp.maximum(old, top_ref[sub, 0:1, :])
            alpha = jnp.exp2(old - new)
            total = sum_ref[sub, 0:1, :] * alpha
            slope = slope_ref[sub, 0:1, :] * alpha
            both = []
            for i, (_, penalty) in enumerate(picked):
                rows = pl.ds(i * BLK, BLK)
                w = jnp.exp2(s_ref[sub, rows, :BLK] * (SCALE * LOG2E) - (new + penalty))
                wt = w * s_ref[sub, rows, BLK:]
                total = total + jnp.sum(w, axis=0, keepdims=True)
                slope = slope + jnp.sum(wt, axis=0, keepdims=True)
                both.append(
                    jnp.concatenate([w.astype(jnp.bfloat16), wt.astype(jnp.bfloat16)], axis=1)
                )
            values = jnp.concatenate([vt_buf[slot] for slot, _ in picked], axis=1)
            out = jnp.dot(values, jnp.concatenate(both, axis=0), preferred_element_type=jnp.float32)
            m_ref[sub, 0:1, :] = new
            sum_ref[sub, 0:1, :] = total
            slope_ref[sub, 0:1, :] = slope
            acc_ref[sub, :HD, :] = acc_ref[sub, :HD, :] * alpha + out[:HD, :BLK]
            acc_ref[sub, HD:, :] = (
                acc_ref[sub, HD:, :] * alpha + out[:HD, BLK:] * SCALE + out[HD:, :BLK]
            )

        def step(n, carry, absorb=absorb, score=score):
            absorb(0, n)
            absorb(1, n)
            score(0, n + 1)
            score(1, n + 1)
            return carry

        steps = (jnp.maximum(ends[0][-1], ends[1][-1]) + group - 1) // group
        score(0, 0)
        score(1, 0)
        lax.fori_loop(0, steps - 1, step, 0)
        absorb(0, steps - 1)
        absorb(1, steps - 1)

        for sub in range(2):
            if not job.final:
                state_out[place * 2 + sub, 0:8, :] = m_ref[sub]
                state_out[place * 2 + sub, 8:16, :] = sum_ref[sub]
                state_out[place * 2 + sub, 16:24, :] = slope_ref[sub]
                state_out[place * 2 + sub, 24:280, :] = acc_ref[sub]
                continue
            out_ref = out_refs[nth]
            total = sum_ref[sub, 0:1, :]
            inv = 1.0 / total
            slope = slope_ref[sub, 0:1, :] * (inv * SCALE)
            o = acc_ref[sub, :HD, :] * inv
            t = acc_ref[sub, HD:, :] * inv - slope * o
            rows = split3(m_ref[sub, 0:1, :]) + split3(total) + split3(slope)
            rows.append(jnp.zeros((STAT - 9, BLK), jnp.float32))
            base = sub * PART
            out_ref[pl.ds(base, HD), :] = o.astype(jnp.bfloat16)
            out_ref[pl.ds(base + HD, HD), :] = t.astype(jnp.bfloat16)
            out_ref[pl.ds(base + 2 * HD, STAT), :] = jnp.concatenate(rows, axis=0).astype(jnp.bfloat16)


def stats_of(ref, base):
    stats = ref[pl.ds(base + 2 * HD, STAT), :].astype(jnp.float32)
    return [stats[3 * i:3 * i + 1] + stats[3 * i + 1:3 * i + 2] + stats[3 * i + 2:3 * i + 3] for i in range(3)]


def weigh(peaks, totals, slopes):
    peak = peaks[0]
    for p in peaks[1:]:
        peak = jnp.maximum(peak, p)
    shares = [l * jnp.exp2(p - peak) for l, p in zip(totals, peaks)]
    total = sum(shares[1:], shares[0])
    inv = 1.0 / total
    shares = [a * inv for a in shares]
    slope = sum((a * s for a, s in zip(shares[1:], slopes[1:])), shares[0] * slopes[0])
    return peak, total, slope, shares


def gather_kernel(*refs):
    part_refs, (o_ref, t_ref, stat_ref) = refs[:-3], refs[-3:]
    for sub in range(2):
        base = sub * PART
        peaks, totals, slopes = zip(*(stats_of(ref, base) for ref in part_refs))
        peak, total, slope, shares = weigh(peaks, totals, slopes)
        o = jnp.zeros((HD, BLK), jnp.float32)
        t = jnp.zeros((HD, BLK), jnp.float32)
        for ref, a, s in zip(part_refs, shares, slopes):
            oj = ref[pl.ds(base, HD), :].astype(jnp.float32)
            tj = ref[pl.ds(base + HD, HD), :].astype(jnp.float32)
            o = o + a * oj
            t = t + a * tj + (a * (s - slope)) * oj
        o_ref[sub] = o
        t_ref[sub] = t
        stat_ref[sub] = jnp.concatenate([peak, total, slope, jnp.zeros((5, BLK), jnp.float32)], axis=0)


def combine_kernel(o_in, t_in, stat_in, *refs):
    part_refs, (o_ref, t_ref) = refs[:-2], refs[-2:]
    for sub in range(2):
        base = sub * PART
        peaks, totals, slopes = zip(*(stats_of(ref, base) for ref in part_refs))
        first = [stat_in[sub, i:i + 1, :] for i in range(3)]
        peaks, totals, slopes = (first[0],) + peaks, (first[1],) + totals, (first[2],) + slopes
        _, _, slope, shares = weigh(peaks, totals, slopes)
        o = shares[0] * o_in[sub]
        t = shares[0] * t_in[sub] + (shares[0] * (slopes[0] - slope)) * o_in[sub]
        for ref, a, s in zip(part_refs, shares[1:], slopes[1:]):
            oj = ref[pl.ds(base, HD), :].astype(jnp.float32)
            tj = ref[pl.ds(base + HD, HD), :].astype(jnp.float32)
            o = o + a * oj
            t = t + a * tj + (a * (s - slope)) * oj
        o_ref[pl.ds(sub * BLK, BLK), :] = o.T.astype(jnp.bfloat16)
        t_ref[pl.ds(sub * BLK, BLK), :] = t.T.astype(jnp.bfloat16)


def shift(size, k):
    return [(i, (i + k) % size) for i in range(size)]


def attend(job, me, tables, *arrays):
    smem = pl.BlockSpec(memory_space=pltpu.SMEM)
    vmem = pl.BlockSpec(memory_space=pltpu.VMEM)
    anywhere = pl.BlockSpec(memory_space=pl.ANY)
    count, n_shards, n_out = len(job.slabs), 4 * len(job.slabs), len(job.places)
    shape = jax.ShapeDtypeStruct
    k_shape, v_shape = (n_shards * 2 * BLK, 2 * HD), (n_shards * 2, 2 * HD, BLK)
    in_specs = [smem] + [anywhere] * count
    in_specs += [anywhere] * 4 if job.fresh else [vmem] * 2
    in_specs += [anywhere] * len(job.pieces) if job.pieces else [vmem] * 2
    if job.fresh:
        outs = [shape((16, 2 * HD, 2 * BLK), jnp.bfloat16), shape((16, 24 + 2 * HD, BLK), jnp.float32)]
    else:
        outs = [shape((2 * PART, BLK), jnp.bfloat16)] * n_out
    if job.keep:
        outs = outs + [shape(k_shape, jnp.bfloat16), shape(v_shape, jnp.bfloat16)]
    scratch = [
        pltpu.SMEM((count, 16, 128), jnp.int32),
        pltpu.VMEM((2, job.group * BLK, 2 * BLK), jnp.float32),
        pltpu.VMEM((2, 8, BLK), jnp.float32),
        pltpu.VMEM((2, 8, BLK), jnp.float32),
        pltpu.VMEM((2, 8, BLK), jnp.float32),
        pltpu.VMEM((2, 8, BLK), jnp.float32),
        pltpu.VMEM((2, 2 * HD, BLK), jnp.float32),
        pltpu.SemaphoreType.DMA((count,)),
    ]
    if job.fresh:
        scratch += [pltpu.VMEM((4, 4 * TOK, HD), jnp.bfloat16), pltpu.SemaphoreType.DMA((4,))]
    if job.pieces:
        scratch += [
            pltpu.VMEM((n_shards * 4 * TOK, HD), jnp.bfloat16),
            pltpu.SemaphoreType.DMA((len(job.pieces),)),
        ]
        if not job.keep:
            scratch += [pltpu.VMEM(k_shape, jnp.bfloat16), pltpu.VMEM(v_shape, jnp.bfloat16)]
    pairs = 2 * n_out * count * 4
    return pl.pallas_call(
        functools.partial(attend_kernel, job),
        out_shape=outs,
        in_specs=in_specs,
        out_specs=[vmem] * len(outs),
        scratch_shapes=scratch,
        compiler_params=pltpu.CompilerParams(vmem_limit_bytes=job.room * 2**20),
        cost_estimate=pl.CostEstimate(
            flops=pairs * 60_000_000, bytes_accessed=4 * 2**20, transcendentals=pairs * BLK * BLK
        ),
        name=job.name,
    )(me, *tables, *arrays)


def shards(q, qt, k, v, kt, vt, block_list, block_count):
    me = jnp.stack([lax.axis_index(a) for a in ("yl", "c", "x", "yh", "z")]).astype(jnp.int32)
    flip = [(0, 1), (1, 0)]
    shard = 4 * TOK

    own = jnp.concatenate([k, kt, v, vt], axis=0)
    pair = jnp.concatenate([own, lax.ppermute(own, "yl", flip)], axis=0)
    table = jnp.concatenate([block_list[:, 0, :], block_count, jnp.zeros((64, 119), jnp.int32)], axis=1)
    tables = [table] + [lax.ppermute(table, "x", shift(NX, d)) for d in (1, 2, 3)]
    pair, *tables = lax.optimization_barrier((pair, *tables))
    ahead = lax.ppermute(pair, "x", shift(NX, 1))
    behind = lax.ppermute(pair, "x", shift(NX, 3))
    far0 = lax.ppermute(ahead[:shard], "x", shift(NX, 1))
    far1 = lax.ppermute(behind[shard:], "x", shift(NX, 3))
    mine = [pair, ahead, behind]
    theirs = [lax.ppermute(a, "c", flip) for a in mine]

    asked = jnp.concatenate([q, qt], axis=0)
    asked = jnp.concatenate([asked, lax.ppermute(asked, "yh", flip)], axis=0)
    queries = [asked] + [lax.ppermute(asked, "z", shift(NZ, d)) for d in (1, 2, 3)]

    near = Job("near", (0,), tuple(range(8)), [(0, 2), (2, 2)], True, False, False, 4, 12)
    pieces = [((dx - 1) * 4 + dc * 2 + dyl, n) for dc in range(2) for dx, dyl, n in PIECES]
    away = Job("away", (1, 2, 3), (4, 5, 6, 7), pieces, False, True, True, GROUP, 20)
    home = Job("home", (1, 2, 3), (0, 1, 2, 3), [], False, True, False, GROUP, 12)
    wq, state = attend(near, me, tables[:1], *queries, mine[0], theirs[0])
    far0, far1, wq, state = lax.optimization_barrier((far0, far1, wq, state))
    far = [far0, far1]
    mine = mine[1:] + far
    theirs = theirs[1:] + [lax.ppermute(a, "c", flip) for a in far]
    *outer, k_buf, vt_buf = attend(away, me, tables[1:], wq, state, *mine, *theirs)
    inner = attend(home, me, tables[1:], wq, state, k_buf, vt_buf)
    parts = list(inner) + list(outer)

    back = [parts[0]]
    for place in range(1, 8):
        dyh, dz = place // 4, place % 4
        route = [
            ((yh ^ dyh) * NZ + (z + dz) % NZ, yh * NZ + z) for yh in range(2) for z in range(NZ)
        ]
        back.append(lax.ppermute(parts[place], ("yh", "z"), route))
    vmem = pl.BlockSpec(memory_space=pltpu.VMEM)
    some = pl.pallas_call(
        gather_kernel,
        out_shape=[jax.ShapeDtypeStruct((2, n, BLK), jnp.float32) for n in (HD, HD, 8)],
        in_specs=[vmem] * 4,
        out_specs=[vmem] * 3,
        compiler_params=pltpu.CompilerParams(vmem_limit_bytes=8 * 2**20),
        name="gather",
    )(*back[4:])
    return tuple(
        pl.pallas_call(
            combine_kernel,
            out_shape=[jax.ShapeDtypeStruct((TOK, HD), jnp.bfloat16)] * 2,
            in_specs=[vmem] * 7,
            out_specs=[vmem] * 2,
            compiler_params=pltpu.CompilerParams(vmem_limit_bytes=8 * 2**20),
            name="combine",
        )(*some, *back[:4])
    )


def solution(mesh):
    split = Mesh(np.asarray(mesh.devices).reshape(2, 2, NX, 2, NZ), ("yl", "c", "x", "yh", "z"))
    pb, kv = ("yl", "c"), ("x", "yh", "z")
    row = P(pb + kv, None)
    return jax.shard_map(
        shards,
        mesh=split,
        in_specs=(row,) * 6 + (P(pb, kv, None), P(pb, kv)),
        out_specs=(row, row),
        check_vma=False,
    )
```

time: 112 us -> 91.5 us (0.82)
  waiting for transfers between devices: 37 us -> 22.4 us
  Pallas kernels: 27.6 us -> 22.1 us
  starting transfers between devices: 38.6 us -> 37.3 us
    ppermute x1, waiting for transfers between devices: 8.36 us -> 2.22 us  [shards(): pair = jnp.concatenate([own, lax.ppermute(own, 'yl', flip)], axis=0)]
    ppermute x1, waiting for transfers between devices: 0.96 us -> 6.77 us  [shards(): ahead = lax.ppermute(pair, 'x', shift(NX, 1))]
    pallas_call x1 -> x4, Pallas kernels: 26.5 us -> 21.2 us  [the longest x3 21 us: attend(): pl.pallas_call(functools.partial(attend_kernel, job), out_shape=outs, in_...]
    ppermute x1, waiting for transfers between devices: 5 us -> 0.01 us  [shards(): behind = lax.ppermute(pair, 'x', shift(NX, 3))]
    ppermute x7, waiting for transfers between devices: 10.6 us -> 6.04 us  [shards(): back.append(lax.ppermute(parts[place], ('yh', 'z'), route))]
    ppermute x3, waiting for transfers between devices: 3.93 us -> 0.01 us  [shards(): lax.ppermute(table, 'x', shift(NX, d))]
    ppermute x1, waiting for transfers between devices: 3.67 us -> 0.01 us  [shards(): far0 = lax.ppermute(ahead[:shard], 'x', shift(NX, 1))]
    ppermute x3, waiting for transfers between devices: 0.01 us -> 3.51 us  [shards(): lax.ppermute(asked, 'z', shift(NZ, d))]
  transfers between devices with their start and end apart: 24 -> 24, of which waited for: 11 -> 10; matrix products, arithmetic and copies ran while one was open for 1% -> 7% of each run, Pallas kernels for 0% -> 16%
where the time goes in v1:
time: 91.5 us; the launch traced here: 90.5 us
  starting transfers between devices  37.3 us (41%)
  waiting for transfers between devices  22.4 us (24%)
  Pallas kernels  22.1 us (24%)
  local copies, waits for them, and re-layouts  6.03 us (7%)
  other arithmetic  1.91 us (2%)
    pallas_call x3, Pallas kernels, attend(): pl.pallas_call(functools.partial(attend_kernel, job), out_shape=outs, in_...  21 us
    ppermute x7, starting transfers between devices, shards(): back.append(lax.ppermute(parts[place], ('yh', 'z'), route))  18.3 us
    ppermute x1, waiting for transfers between devices, shards(): ahead = lax.ppermute(pair, 'x', shift(NX, 1))  6.77 us
    ppermute x7, waiting for transfers between devices, shards(): back.append(lax.ppermute(parts[place], ('yh', 'z'), route))  6.04 us
    unnamed x10, local copies, waits for them, and re-layouts  5.78 us
    ppermute x3, starting transfers between devices, shards(): lax.ppermute(asked, 'z', shift(NZ, d))  5.37 us
    ppermute x3, starting transfers between devices, shards(): lax.ppermute(table, 'x', shift(NX, d))  4.54 us
    ppermute x3, waiting for transfers between devices, shards(): lax.ppermute(asked, 'z', shift(NZ, d))  3.51 us
  transfers between devices with their start and end apart: 24, of which 10 were waited for; matrix products, arithmetic and copies ran while one was open for 7% of the time, Pallas kernels for 16%

profile of v1, /device:TPU:0, one launch (start us, length us, event | category | flops | bytes accessed | tf_op | source)
XLA Modules:
  0.0 90.5 jit_solution(8628356197400921984)
XLA Ops:
  2.3 2.9 %collective-permute-start.3 = (s32[64,128]{1,0:T(8,128)S(1)}, s32[64,128]{1,0:T(8,128)S(1)}, u32[]{:S(2)}, u32[]{:S(2)}) collective-permute-start(s32[64,128]{1,0:T(8,128)S(1)} %add_add_fusion.refs_0_), channel_id=1, source_target_pairs={{0,24},{8,0},{16,8},{24,16},{1,25},{9,1},{17,9},{25,17},{2,26},{10... | collective-permute-start | bytes 98312 | tf_op jit(solution)/shard_map/ppermute | solution.py:339
  7.8 1.7 %collective-permute-start = (bf16[1024,128]{1,0:T(8,128)(2,1)S(1)}, bf16[1024,128]{1,0:T(8,128)(2,1)S(1)}, u32[]{:S(2)}, u32[]{:S(2)}) collective-permute-start(bf16[1024,128]{1,0:T(8,128)(2,1)S(1)} %pad_maximum_fusion), channel_id=1, source_target_pairs={{0,64},{64,0},{1,65},{65,1},{2,66},{66,2},{3,67},{67,3},{4,68},{68... | collective-permute-start | bytes 786440 | tf_op jit(solution)/shard_map/ppermute | solution.py:337
  12.9 2.2 %collective-permute-done = bf16[1024,128]{1,0:T(8,128)(2,1)S(1)} collective-permute-done((bf16[1024,128]{1,0:T(8,128)(2,1)S(1)}, bf16[1024,128]{1,0:T(8,128)(2,1)S(1)}, u32[]{:S(2)}, u32[]{:S(2)}) %collective-permute-start) | collective-permute-done | bytes 262176 | tf_op jit(solution)/shard_map/ppermute | solution.py:337
  15.2 2.4 %collective-permute-start.6 = (bf16[2048,128]{1,0:T(8,128)(2,1)S(1)}, bf16[2048,128]{1,0:T(8,128)(2,1)S(1)}, u32[]{:S(2)}, u32[]{:S(2)}) collective-permute-start(bf16[2048,128]{1,0:T(8,128)(2,1)S(1)} %constant_dynamic-update-slice_fusion.refs_5_), channel_id=1, source_target_pairs={{0,24},{8,0},{16,8},{24,16},{1,25},{9,1},{17,9},{25,17},{2,26},{10... | collective-permute-start | bytes 1572872 | tf_op jit(solution)/shard_map/ppermute | solution.py:342
  18.5 3.3 %collective-permute-start.8 = (bf16[512,128]{1,0:T(8,128)(2,1)S(1)}, bf16[512,128]{1,0:T(8,128)(2,1)S(1)}, u32[]{:S(2)}, u32[]{:S(2)}) collective-permute-start(bf16[512,128]{1,0:T(8,128)(2,1)S(1)} %pad_maximum_fusion.1), channel_id=1, source_target_pairs={{0,4},{4,0},{1,5},{5,1},{2,6},{6,2},{3,7},{7,3},{8,12},{12,8},{9,1... | collective-permute-start | bytes 393224 | tf_op jit(solution)/shard_map/ppermute | solution.py:349
  22.6 2.4 %collective-permute-done.8 = bf16[512,128]{1,0:T(8,128)(2,1)S(1)} collective-permute-done((bf16[512,128]{1,0:T(8,128)(2,1)S(1)}, bf16[512,128]{1,0:T(8,128)(2,1)S(1)}, u32[]{:S(2)}, u32[]{:S(2)}) %collective-permute-start.8) | collective-permute-done | bytes 131104 | tf_op jit(solution)/shard_map/ppermute | solution.py:349
  25.0 4.1 %collective-permute-start.11 = (bf16[1024,128]{1,0:T(8,128)(2,1)S(1)}, bf16[1024,128]{1,0:T(8,128)(2,1)S(1)}, u32[]{:S(2)}, u32[]{:S(2)}) collective-permute-start(bf16[1024,128]{1,0:T(8,128)(2,1)S(1)} %constant_dynamic-update-slice_fusion.5.refs_1_), channel_id=1, source_target_pairs={{0,3},{1,0},{2,1},{3,2},{4,7},{5,4},{6,5},{7,6},{8,11},{9,8},{10,9... | collective-permute-start | bytes 786440 | tf_op jit(solution)/shard_map/ppermute | solution.py:350
  29.2 1.3 %collective-permute-start.9 = (bf16[1024,128]{1,0:T(8,128)(2,1)S(1)}, bf16[1024,128]{1,0:T(8,128)(2,1)S(1)}, u32[]{:S(2)}, u32[]{:S(2)}) collective-permute-start(bf16[1024,128]{1,0:T(8,128)(2,1)S(1)} %constant_dynamic-update-slice_fusion.5.refs_1_), channel_id=1, source_target_pairs={{0,1},{1,2},{2,3},{3,0},{4,5},{5,6},{6,7},{7,4},{8,9},{9,10},{10,1... | collective-permute-start | bytes 786440 | tf_op jit(solution)/shard_map/ppermute | solution.py:350
  30.5 6.8 %collective-permute-done.4.refs_5_ = bf16[2048,128]{1,0:T(8,128)(2,1)S(1)} collective-permute-done((bf16[2048,128]{1,0:T(8,128)(2,1)S(1)}, bf16[2048,128]{1,0:T(8,128)(2,1)S(1)}, u32[]{:S(2)}, u32[]{:S(2)}) %collective-permute-start.4) | collective-permute-done | bytes 524320 | tf_op jit(solution)/shard_map/ppermute | solution.py:341
  37.3 1.3 %collective-permute-done.11.refs_4_ = bf16[1024,128]{1,0:T(8,128)(2,1)S(1)} collective-permute-done((bf16[1024,128]{1,0:T(8,128)(2,1)S(1)}, bf16[1024,128]{1,0:T(8,128)(2,1)S(1)}, u32[]{:S(2)}, u32[]{:S(2)}) %collective-permute-start.11) | collective-permute-done | bytes 262176 | tf_op jit(solution)/shard_map/ppermute | solution.py:350
  38.6 1.2 %collective-permute-start.5 = (bf16[1024,128]{1,0:T(8,128)(2,1)S(1)}, bf16[1024,128]{1,0:T(8,128)(2,1)S(1)}, u32[]{:S(2)}, u32[]{:S(2)}) collective-permute-start(bf16[1024,128]{1,0:T(8,128)(2,1)S(1)} %slice.8), channel_id=1, source_target_pairs={{0,8},{8,16},{16,24},{24,0},{1,9},{9,17},{17,25},{25,1},{2,10},{10... | collective-permute-start | bytes 786440 | tf_op jit(solution)/shard_map/ppermute | solution.py:343
  39.8 2.2 %collective-permute-done.9.refs_2_ = bf16[1024,128]{1,0:T(8,128)(2,1)S(1)} collective-permute-done((bf16[1024,128]{1,0:T(8,128)(2,1)S(1)}, bf16[1024,128]{1,0:T(8,128)(2,1)S(1)}, u32[]{:S(2)}, u32[]{:S(2)}) %collective-permute-start.9) | collective-permute-done | bytes 262176 | tf_op jit(solution)/shard_map/ppermute | solution.py:350
  42.0 7.9 %near.1 = (bf16[16,256,256]{2,1,0:T(8,128)(2,1)S(1)}, f32[16,280,128]{2,1,0:T(8,128)S(1)}) custom-call(s32[5]{0:T(128)S(1)} %stack.23.me_ref, s32[64,128]{1,0:T(8,128)S(1)} %add_add_fusion.refs_0_, bf16[1024,128]{1,0:T(8,128)(2,1)S(1)} %constant_dynamic-update-slice_fusion.5.refs_1_, bf16[1024,128]{1,0:T(8,128)(2,1)S(1)} %collective-permute-done.9.refs_2_, ...), custom_call_target="tpu_custom_call" | custom-call | flops 3840000000 | bytes 4194304 | tf_op jit(solution)/shard_map/near/pallas_call | solution.py:317
  50.6 1.0 %collective-permute-done.15.refs_11_ = bf16[1024,128]{1,0:T(8,128)(2,1)S(1)} collective-permute-done((bf16[1024,128]{1,0:T(8,128)(2,1)S(1)}, bf16[1024,128]{1,0:T(8,128)(2,1)S(1)}, u32[]{:S(2)}, u32[]{:S(2)}) %collective-permute-start.15) | collective-permute-done | bytes 262176 | tf_op jit(solution)/shard_map/ppermute | solution.py:360
  51.9 7.0 %away.1 = (bf16[544,128]{1,0:T(8,128)(2,1)S(1)}, bf16[544,128]{1,0:T(8,128)(2,1)S(1)}, bf16[544,128]{1,0:T(8,128)(2,1)S(1)}, bf16[544,128]{1,0:T(8,128)(2,1)S(1)...) custom-call(s32[5]{0:T(128)S(1)} %stack.23.me_ref, s32[64,128]{1,0:T(8,128)S(1)} %collective-permute-done.1.refs_0_, ...), custom_call_target="tpu_custom_call" | custom-call | flops 5760000000 | bytes 4194304 | tf_op jit(solution)/shard_map/away/pallas_call | solution.py:317
  59.9 6.1 %collective-permute-start.18 = (bf16[544,128]{1,0:T(8,128)(2,1)S(1)}, bf16[544,128]{1,0:T(8,128)(2,1)S(1)}, u32[]{:S(2)}, u32[]{:S(2)}) collective-permute-start(bf16[544,128]{1,0:T(8,128)(2,1)S(1)} %get-tuple-element.38), channel_id=1, source_target_pairs={{5,0},{6,1},{7,2},{4,3},{1,4},{2,5},{3,6},{0,7},{13,8},{14,9},{15,... | collective-permute-start | bytes 417800 | tf_op jit(solution)/shard_map/ppermute | solution.py:371
  66.0 1.0 %collective-permute-start.19 = (bf16[544,128]{1,0:T(8,128)(2,1)S(1)}, bf16[544,128]{1,0:T(8,128)(2,1)S(1)}, u32[]{:S(2)}, u32[]{:S(2)}) collective-permute-start(bf16[544,128]{1,0:T(8,128)(2,1)S(1)} %get-tuple-element.39), channel_id=1, source_target_pairs={{6,0},{7,1},{4,2},{5,3},{2,4},{3,5},{0,6},{1,7},{14,8},{15,9},{12,... | collective-permute-start | bytes 417800 | tf_op jit(solution)/shard_map/ppermute | solution.py:371
  67.0 1.1 %collective-permute-start.20 = (bf16[544,128]{1,0:T(8,128)(2,1)S(1)}, bf16[544,128]{1,0:T(8,128)(2,1)S(1)}, u32[]{:S(2)}, u32[]{:S(2)}) collective-permute-start(bf16[544,128]{1,0:T(8,128)(2,1)S(1)} %get-tuple-element.40), channel_id=1, source_target_pairs={{7,0},{4,1},{5,2},{6,3},{3,4},{0,5},{1,6},{2,7},{15,8},{12,9},{13,... | collective-permute-start | bytes 417800 | tf_op jit(solution)/shard_map/ppermute | solution.py:371
  68.1 6.1 %home.1 = (bf16[544,128]{1,0:T(8,128)(2,1)S(1)}, bf16[544,128]{1,0:T(8,128)(2,1)S(1)}, bf16[544,128]{1,0:T(8,128)(2,1)S(1)}, bf16[544,128]{1,0:T(8,128)(2,1)S(1)}) custom-call(s32[5]{0:T(128)S(1)} %stack.23.me_ref, s32[64,128]{1,0:T(8,128)S(1)} %collective-permute-done.1.refs_0_, s32[64,128]{1,0:T(8,128)S(1)} %collective-permute-done.2.refs_1_, ...), custom_call_target="tpu_custom_call" | custom-call | flops 5760000000 | bytes 4194304 | tf_op jit(solution)/shard_map/home/pallas_call | solution.py:317
  74.3 6.2 %collective-permute-start.21 = (bf16[544,128]{1,0:T(8,128)(2,1)S(1)}, bf16[544,128]{1,0:T(8,128)(2,1)S(1)}, u32[]{:S(2)}, u32[]{:S(2)}) collective-permute-start(bf16[544,128]{1,0:T(8,128)(2,1)S(1)} %get-tuple-element.47), channel_id=1, source_target_pairs={{1,0},{2,1},{3,2},{0,3},{5,4},{6,5},{7,6},{4,7},{9,8},{10,9},{11,1... | collective-permute-start | bytes 417800 | tf_op jit(solution)/shard_map/ppermute | solution.py:371
  80.4 2.9 %collective-permute-start.22 = (bf16[544,128]{1,0:T(8,128)(2,1)S(1)}, bf16[544,128]{1,0:T(8,128)(2,1)S(1)}, u32[]{:S(2)}, u32[]{:S(2)}) collective-permute-start(bf16[544,128]{1,0:T(8,128)(2,1)S(1)} %get-tuple-element.48), channel_id=1, source_target_pairs={{2,0},{3,1},{0,2},{1,3},{6,4},{7,5},{4,6},{5,7},{10,8},{11,9},{8,1... | collective-permute-start | bytes 417800 | tf_op jit(solution)/shard_map/ppermute | solution.py:371
  83.6 2.2 %collective-permute-done.21.refs_1_ = bf16[544,128]{1,0:T(8,128)(2,1)S(1)} collective-permute-done((bf16[544,128]{1,0:T(8,128)(2,1)S(1)}, bf16[544,128]{1,0:T(8,128)(2,1)S(1)}, u32[]{:S(2)}, u32[]{:S(2)}) %collective-permute-start.21) | collective-permute-done | bytes 139296 | tf_op jit(solution)/shard_map/ppermute | solution.py:371
  85.8 2.2 %collective-permute-done.22.refs_2_ = bf16[544,128]{1,0:T(8,128)(2,1)S(1)} collective-permute-done((bf16[544,128]{1,0:T(8,128)(2,1)S(1)}, bf16[544,128]{1,0:T(8,128)(2,1)S(1)}, u32[]{:S(2)}, u32[]{:S(2)}) %collective-permute-start.22) | collective-permute-done | bytes 139296 | tf_op jit(solution)/shard_map/ppermute | solution.py:371
  88.0 1.6 %collective-permute-done.23.refs_3_ = bf16[544,128]{1,0:T(8,128)(2,1)S(1)} collective-permute-done((bf16[544,128]{1,0:T(8,128)(2,1)S(1)}, bf16[544,128]{1,0:T(8,128)(2,1)S(1)}, u32[]{:S(2)}, u32[]{:S(2)}) %collective-permute-start.23) | collective-permute-done | bytes 139296 | tf_op jit(solution)/shard_map/ppermute | solution.py:371
  (49 shorter events, 12.8 us)
Async XLA Ops:
  2.3 12.8 %collective-permute-start.3 = (s32[64,128]{1,0:T(8,128)S(1)}, s32[64,128]{1,0:T(8,128)S(1)}, u32[]{:S(2)}, u32[]{:S(2)}) collective-permute-start(s32[64,128]{1,0:T(8,128)S(1)} %add_add_fusion.refs_0_), channel_id=1, source_target_pairs={{0,24},{8,0},{16,8},{24,16},{1,25},{9,1},{17,9},{25,17},{2,26},{10... | collective-permute-start | bytes 98312 | tf_op jit(solution)/shard_map/ppermute | solution.py:339
  5.2 10.0 %collective-permute-start.2 = (s32[64,128]{1,0:T(8,128)S(1)}, s32[64,128]{1,0:T(8,128)S(1)}, u32[]{:S(2)}, u32[]{:S(2)}) collective-permute-start(s32[64,128]{1,0:T(8,128)S(1)} %add_add_fusion.refs_0_), channel_id=1, source_target_pairs={{0,16},{8,24},{16,0},{24,8},{1,17},{9,25},{17,1},{25,9},{2,18},{10... | collective-permute-start | bytes 98312 | tf_op jit(solution)/shard_map/ppermute | solution.py:339
  6.0 9.2 %collective-permute-start.1 = (s32[64,128]{1,0:T(8,128)S(1)}, s32[64,128]{1,0:T(8,128)S(1)}, u32[]{:S(2)}, u32[]{:S(2)}) collective-permute-start(s32[64,128]{1,0:T(8,128)S(1)} %add_add_fusion.refs_0_), channel_id=1, source_target_pairs={{0,8},{8,16},{16,24},{24,0},{1,9},{9,17},{17,25},{25,1},{2,10},{10... | collective-permute-start | bytes 98312 | tf_op jit(solution)/shard_map/ppermute | solution.py:339
  7.8 7.3 %collective-permute-start = (bf16[1024,128]{1,0:T(8,128)(2,1)S(1)}, bf16[1024,128]{1,0:T(8,128)(2,1)S(1)}, u32[]{:S(2)}, u32[]{:S(2)}) collective-permute-start(bf16[1024,128]{1,0:T(8,128)(2,1)S(1)} %pad_maximum_fusion), channel_id=1, source_target_pairs={{0,64},{64,0},{1,65},{65,1},{2,66},{66,2},{3,67},{67,3},{4,68},{68... | collective-permute-start | bytes 786440 | tf_op jit(solution)/shard_map/ppermute | solution.py:337
  15.2 14.0 %collective-permute-start.6 = (bf16[2048,128]{1,0:T(8,128)(2,1)S(1)}, bf16[2048,128]{1,0:T(8,128)(2,1)S(1)}, u32[]{:S(2)}, u32[]{:S(2)}) collective-permute-start(bf16[2048,128]{1,0:T(8,128)(2,1)S(1)} %constant_dynamic-update-slice_fusion.refs_5_), channel_id=1, source_target_pairs={{0,24},{8,0},{16,8},{24,16},{1,25},{9,1},{17,9},{25,17},{2,26},{10... | collective-permute-start | bytes 1572872 | tf_op jit(solution)/shard_map/ppermute | solution.py:342
  18.5 6.6 %collective-permute-start.8 = (bf16[512,128]{1,0:T(8,128)(2,1)S(1)}, bf16[512,128]{1,0:T(8,128)(2,1)S(1)}, u32[]{:S(2)}, u32[]{:S(2)}) collective-permute-start(bf16[512,128]{1,0:T(8,128)(2,1)S(1)} %pad_maximum_fusion.1), channel_id=1, source_target_pairs={{0,4},{4,0},{1,5},{5,1},{2,6},{6,2},{3,7},{7,3},{8,12},{12,8},{9,1... | collective-permute-start | bytes 393224 | tf_op jit(solution)/shard_map/ppermute | solution.py:349
  21.7 20.3 %collective-permute-start.12 = (bf16[2048,128]{1,0:T(8,128)(2,1)S(1)}, bf16[2048,128]{1,0:T(8,128)(2,1)S(1)}, u32[]{:S(2)}, u32[]{:S(2)}) collective-permute-start(bf16[2048,128]{1,0:T(8,128)(2,1)S(1)} %constant_dynamic-update-slice_fusion.refs_5_), channel_id=1, source_target_pairs={{0,32},{32,0},{1,33},{33,1},{2,34},{34,2},{3,35},{35,3},{4,36},{36... | collective-permute-start | bytes 1572872 | tf_op jit(solution)/shard_map/ppermute | solution.py:346
  21.8 15.5 %collective-permute-start.4 = (bf16[2048,128]{1,0:T(8,128)(2,1)S(1)}, bf16[2048,128]{1,0:T(8,128)(2,1)S(1)}, u32[]{:S(2)}, u32[]{:S(2)}) collective-permute-start(bf16[2048,128]{1,0:T(8,128)(2,1)S(1)} %constant_dynamic-update-slice_fusion.refs_5_), channel_id=1, source_target_pairs={{0,8},{8,16},{16,24},{24,0},{1,9},{9,17},{17,25},{25,1},{2,10},{10... | collective-permute-start | bytes 1572872 | tf_op jit(solution)/shard_map/ppermute | solution.py:341
  25.0 13.6 %collective-permute-start.11 = (bf16[1024,128]{1,0:T(8,128)(2,1)S(1)}, bf16[1024,128]{1,0:T(8,128)(2,1)S(1)}, u32[]{:S(2)}, u32[]{:S(2)}) collective-permute-start(bf16[1024,128]{1,0:T(8,128)(2,1)S(1)} %constant_dynamic-update-slice_fusion.5.refs_1_), channel_id=1, source_target_pairs={{0,3},{1,0},{2,1},{3,2},{4,7},{5,4},{6,5},{7,6},{8,11},{9,8},{10,9... | collective-permute-start | bytes 786440 | tf_op jit(solution)/shard_map/ppermute | solution.py:350
  29.2 10.7 %collective-permute-start.10 = (bf16[1024,128]{1,0:T(8,128)(2,1)S(1)}, bf16[1024,128]{1,0:T(8,128)(2,1)S(1)}, u32[]{:S(2)}, u32[]{:S(2)}) collective-permute-start(bf16[1024,128]{1,0:T(8,128)(2,1)S(1)} %constant_dynamic-update-slice_fusion.5.refs_1_), channel_id=1, source_target_pairs={{0,2},{1,3},{2,0},{3,1},{4,6},{5,7},{6,4},{7,5},{8,10},{9,11},{10,... | collective-permute-start | bytes 786440 | tf_op jit(solution)/shard_map/ppermute | solution.py:350
  29.2 12.9 %collective-permute-start.9 = (bf16[1024,128]{1,0:T(8,128)(2,1)S(1)}, bf16[1024,128]{1,0:T(8,128)(2,1)S(1)}, u32[]{:S(2)}, u32[]{:S(2)}) collective-permute-start(bf16[1024,128]{1,0:T(8,128)(2,1)S(1)} %constant_dynamic-update-slice_fusion.5.refs_1_), channel_id=1, source_target_pairs={{0,1},{1,2},{2,3},{3,0},{4,5},{5,6},{6,7},{7,4},{8,9},{9,10},{10,1... | collective-permute-start | bytes 786440 | tf_op jit(solution)/shard_map/ppermute | solution.py:350
  37.3 12.6 %collective-permute-start.7 = (bf16[1024,128]{1,0:T(8,128)(2,1)S(1)}, bf16[1024,128]{1,0:T(8,128)(2,1)S(1)}, u32[]{:S(2)}, u32[]{:S(2)}) collective-permute-start(bf16[1024,128]{1,0:T(8,128)(2,1)S(1)} %slice.9), channel_id=1, source_target_pairs={{0,24},{8,0},{16,8},{24,16},{1,25},{9,1},{17,9},{25,17},{2,26},{10... | collective-permute-start | bytes 786440 | tf_op jit(solution)/shard_map/ppermute | solution.py:344
  38.6 11.3 %collective-permute-start.5 = (bf16[1024,128]{1,0:T(8,128)(2,1)S(1)}, bf16[1024,128]{1,0:T(8,128)(2,1)S(1)}, u32[]{:S(2)}, u32[]{:S(2)}) collective-permute-start(bf16[1024,128]{1,0:T(8,128)(2,1)S(1)} %slice.8), channel_id=1, source_target_pairs={{0,8},{8,16},{16,24},{24,0},{1,9},{9,17},{17,25},{25,1},{2,10},{10... | collective-permute-start | bytes 786440 | tf_op jit(solution)/shard_map/ppermute | solution.py:343
  39.8 10.7 %collective-permute-start.14 = (bf16[2048,128]{1,0:T(8,128)(2,1)S(1)}, bf16[2048,128]{1,0:T(8,128)(2,1)S(1)}, u32[]{:S(2)}, u32[]{:S(2)}) collective-permute-start(bf16[2048,128]{1,0:T(8,128)(2,1)S(1)} %collective-permute-done.6.refs_6_), channel_id=1, source_target_pairs={{0,32},{32,0},{1,33},{33,1},{2,34},{34,2},{3,35},{35,3},{4,36},{36... | collective-permute-start | bytes 1572872 | tf_op jit(solution)/shard_map/ppermute | solution.py:346
  42.0 8.5 %collective-permute-start.13 = (bf16[2048,128]{1,0:T(8,128)(2,1)S(1)}, bf16[2048,128]{1,0:T(8,128)(2,1)S(1)}, u32[]{:S(2)}, u32[]{:S(2)}) collective-permute-start(bf16[2048,128]{1,0:T(8,128)(2,1)S(1)} %collective-permute-done.4.refs_5_), channel_id=1, source_target_pairs={{0,32},{32,0},{1,33},{33,1},{2,34},{34,2},{3,35},{35,3},{4,36},{36... | collective-permute-start | bytes 1572872 | tf_op jit(solution)/shard_map/ppermute | solution.py:346
  50.0 1.6 %collective-permute-start.15 = (bf16[1024,128]{1,0:T(8,128)(2,1)S(1)}, bf16[1024,128]{1,0:T(8,128)(2,1)S(1)}, u32[]{:S(2)}, u32[]{:S(2)}) collective-permute-start(bf16[1024,128]{1,0:T(8,128)(2,1)S(1)} %collective-permute-done.5.refs_7_), channel_id=1, source_target_pairs={{0,32},{32,0},{1,33},{33,1},{2,34},{34,2},{3,35},{35,3},{4,36},{36... | collective-permute-start | bytes 786440 | tf_op jit(solution)/shard_map/ppermute | solution.py:360
  50.1 1.9 %collective-permute-start.16 = (bf16[1024,128]{1,0:T(8,128)(2,1)S(1)}, bf16[1024,128]{1,0:T(8,128)(2,1)S(1)}, u32[]{:S(2)}, u32[]{:S(2)}) collective-permute-start(bf16[1024,128]{1,0:T(8,128)(2,1)S(1)} %collective-permute-done.7.refs_8_), channel_id=1, source_target_pairs={{0,32},{32,0},{1,33},{33,1},{2,34},{34,2},{3,35},{35,3},{4,36},{36... | collective-permute-start | bytes 786440 | tf_op jit(solution)/shard_map/ppermute | solution.py:360
  58.9 21.5 %collective-permute-start.17 = (bf16[544,128]{1,0:T(8,128)(2,1)S(1)}, bf16[544,128]{1,0:T(8,128)(2,1)S(1)}, u32[]{:S(2)}, u32[]{:S(2)}) collective-permute-start(bf16[544,128]{1,0:T(8,128)(2,1)S(1)} %get-tuple-element.37), channel_id=1, source_target_pairs={{4,0},{5,1},{6,2},{7,3},{0,4},{1,5},{2,6},{3,7},{12,8},{13,9},{14,... | collective-permute-start | bytes 417800 | tf_op jit(solution)/shard_map/ppermute | solution.py:371
  59.9 23.4 %collective-permute-start.18 = (bf16[544,128]{1,0:T(8,128)(2,1)S(1)}, bf16[544,128]{1,0:T(8,128)(2,1)S(1)}, u32[]{:S(2)}, u32[]{:S(2)}) collective-permute-start(bf16[544,128]{1,0:T(8,128)(2,1)S(1)} %get-tuple-element.38), channel_id=1, source_target_pairs={{5,0},{6,1},{7,2},{4,3},{1,4},{2,5},{3,6},{0,7},{13,8},{14,9},{15,... | collective-permute-start | bytes 417800 | tf_op jit(solution)/shard_map/ppermute | solution.py:371
  66.0 17.3 %collective-permute-start.19 = (bf16[544,128]{1,0:T(8,128)(2,1)S(1)}, bf16[544,128]{1,0:T(8,128)(2,1)S(1)}, u32[]{:S(2)}, u32[]{:S(2)}) collective-permute-start(bf16[544,128]{1,0:T(8,128)(2,1)S(1)} %get-tuple-element.39), channel_id=1, source_target_pairs={{6,0},{7,1},{4,2},{5,3},{2,4},{3,5},{0,6},{1,7},{14,8},{15,9},{12,... | collective-permute-start | bytes 417800 | tf_op jit(solution)/shard_map/ppermute | solution.py:371
  67.0 16.3 %collective-permute-start.20 = (bf16[544,128]{1,0:T(8,128)(2,1)S(1)}, bf16[544,128]{1,0:T(8,128)(2,1)S(1)}, u32[]{:S(2)}, u32[]{:S(2)}) collective-permute-start(bf16[544,128]{1,0:T(8,128)(2,1)S(1)} %get-tuple-element.40), channel_id=1, source_target_pairs={{7,0},{4,1},{5,2},{6,3},{3,4},{0,5},{1,6},{2,7},{15,8},{12,9},{13,... | collective-permute-start | bytes 417800 | tf_op jit(solution)/shard_map/ppermute | solution.py:371
  74.3 11.5 %collective-permute-start.21 = (bf16[544,128]{1,0:T(8,128)(2,1)S(1)}, bf16[544,128]{1,0:T(8,128)(2,1)S(1)}, u32[]{:S(2)}, u32[]{:S(2)}) collective-permute-start(bf16[544,128]{1,0:T(8,128)(2,1)S(1)} %get-tuple-element.47), channel_id=1, source_target_pairs={{1,0},{2,1},{3,2},{0,3},{5,4},{6,5},{7,6},{4,7},{9,8},{10,9},{11,1... | collective-permute-start | bytes 417800 | tf_op jit(solution)/shard_map/ppermute | solution.py:371
  80.4 7.6 %collective-permute-start.22 = (bf16[544,128]{1,0:T(8,128)(2,1)S(1)}, bf16[544,128]{1,0:T(8,128)(2,1)S(1)}, u32[]{:S(2)}, u32[]{:S(2)}) collective-permute-start(bf16[544,128]{1,0:T(8,128)(2,1)S(1)} %get-tuple-element.48), channel_id=1, source_target_pairs={{2,0},{3,1},{0,2},{1,3},{6,4},{7,5},{4,6},{5,7},{10,8},{11,9},{8,1... | collective-permute-start | bytes 417800 | tf_op jit(solution)/shard_map/ppermute | solution.py:371
  83.3 6.3 %collective-permute-start.23 = (bf16[544,128]{1,0:T(8,128)(2,1)S(1)}, bf16[544,128]{1,0:T(8,128)(2,1)S(1)}, u32[]{:S(2)}, u32[]{:S(2)}) collective-permute-start(bf16[544,128]{1,0:T(8,128)(2,1)S(1)} %get-tuple-element.49), channel_id=1, source_target_pairs={{3,0},{0,1},{1,2},{2,3},{7,4},{4,5},{5,6},{6,7},{11,8},{8,9},{9,10... | collective-permute-start | bytes 417800 | tf_op jit(solution)/shard_map/ppermute | solution.py:371
  (1 other events, 22.0 us)

commit v2 on v1

v2 whole, which is shorter than its diff:
```python
import functools
import math

import jax
import jax.numpy as jnp
import numpy as np
from jax import lax
from jax.experimental import pallas as pl
from jax.experimental.pallas import tpu as pltpu
from jax.sharding import Mesh
from jax.sharding import PartitionSpec as P

BLK = 128
HD = 128
LMAX = 8
TOK = 256
NX, NZ = 4, 4
GROUP = 8
SCALE = 1.0 / math.sqrt(HD)
LOG2E = math.log2(math.e)
FLOOR = -1.0e30
STAT = 16
PART = 2 * BLK + STAT
PIECES = ((1, 0, 2), (3, 0, 2), (2, 0, 1), (2, 1, 1))


def split3(x):
    hi = x.astype(jnp.bfloat16).astype(jnp.float32)
    mid = (x - hi).astype(jnp.bfloat16).astype(jnp.float32)
    return [hi, mid, x - hi - mid]


class Job:
    def __init__(self, name, slabs, places, pieces, fresh, final, keep, group, room):
        self.name, self.slabs, self.places, self.pieces = name, slabs, places, pieces
        self.fresh, self.final, self.keep, self.group, self.room = fresh, final, keep, group, room


def attend_kernel(job, me_ref, *refs):
    refs = list(refs)

    def take(n):
        out = refs[:n]
        del refs[:n]
        return out

    group, count = job.group, len(job.slabs)
    tables_in = take(count)
    if job.fresh:
        q_refs = take(4)
    else:
        wq_in, state_in = take(2)
    if job.pieces:
        k_refs = take(len(job.pieces))
    else:
        k_buf, vt_buf = take(2)
    if job.fresh:
        wq_out, state_out = take(2)
    else:
        out_refs = take(len(job.places) // 2)
    if job.keep:
        k_buf, vt_buf = take(2)
    tables, s_ref, top_ref, m_ref, sum_ref, slope_ref, acc_ref, t_sem = take(8)
    if job.pieces and not job.keep:
        k_buf, vt_buf = take(2)
    my_yl, my_c, my_x, my_yh, my_z = (me_ref[i] for i in range(5))
    first_row = pl.multiple_of(my_x * 16, 16)

    t_copies = [
        pltpu.make_async_copy(ref.at[pl.ds(first_row, 16), :], tables.at[i], t_sem.at[i])
        for i, ref in enumerate(tables_in)
    ]
    for copy in t_copies:
        copy.start()
    if job.pieces:
        for ref, (at, size) in zip(k_refs, job.pieces):
            for shard in range(size):
                for half in range(2):
                    slot = (at + shard) * 2 + half
                    for part in range(2):
                        rows = pl.ds(shard * 4 * TOK + part * TOK + half * BLK, BLK)
                        k_buf[pl.ds(slot * BLK, BLK), pl.ds(part * HD, HD)] = ref[rows, :]
                        rows = pl.ds(shard * 4 * TOK + (2 + part) * TOK + half * BLK, BLK)
                        vt_buf[slot, pl.ds(part * HD, HD), :] = ref[rows, :].T
    for copy in t_copies:
        copy.wait()
    base_dx = min(job.slabs)

    wq = wq_out if job.fresh else wq_in

    def prepare(nth):
        place, side = job.places[nth], nth % 2
        dyh, dz = place // 4, place % 4
        row0 = (my_yh ^ dyh) * 8 + ((my_z - dz + NZ) & 3) * 2
        ends = []
        for sub in range(2):
            stops, stop = [], jnp.int32(0)
            for i in range(count):
                stop = stop + tables[i, row0 + sub, LMAX]
                stops.append(stop)
            ends.append(stops)
            if job.fresh:
                at = dyh * 2 * TOK + sub * BLK
                qx = q_refs[dz][pl.ds(at, BLK), :].T
                wq_out[place * 2 + sub, HD:, :HD] = jnp.zeros((HD, BLK), jnp.bfloat16)
                wq_out[place * 2 + sub, :HD, :HD] = qx
                wq_out[place * 2 + sub, HD:, HD:] = qx
                wq_out[place * 2 + sub, :HD, HD:] = q_refs[dz][pl.ds(at + TOK, BLK), :].T

        def pick(sub, at):
            stops = ends[sub]
            penalty = jnp.where(at < stops[-1], jnp.float32(0.0), jnp.float32(-FLOOR))
            at = jnp.minimum(at, stops[-1] - 1)
            row = row0 + sub
            g = tables[0, row, jnp.minimum(at, LMAX - 1)]
            for i, stop in enumerate(stops[:-1]):
                g = jnp.where(at >= stop, tables[i + 1, row, jnp.clip(at - stop, 0, LMAX - 1)], g)
            shard = g >> 1
            x, c, yl = (shard >> 3) & 3, (shard >> 5) & 1, (shard >> 6) & 1
            dx = (my_x - x + NX) & 3
            slot = ((((dx - base_dx) * 2 + (c ^ my_c)) * 2) + (yl ^ my_yl)) * 2 + (g & 1)
            return slot, penalty

        def score(sub, n):
            keys = []
            for i in range(group):
                slot, _ = pick(sub, n * group + i)
                keys.append(k_buf[pl.ds(pl.multiple_of(slot * BLK, BLK), BLK), :])
            dots = jnp.dot(
                jnp.concatenate(keys, axis=0), wq[place * 2 + sub], preferred_element_type=jnp.float32
            )
            s_ref[side, sub] = dots
            top_ref[side, sub, 0:1, :] = jnp.max(dots[:, :BLK], axis=0, keepdims=True) * (SCALE * LOG2E)

        def absorb(sub, n):
            picked = [pick(sub, n * group + i) for i in range(group)]
            old = m_ref[side, sub, 0:1, :]
            new = jnp.maximum(old, top_ref[side, sub, 0:1, :])
            alpha = jnp.exp2(old - new)
            total = sum_ref[side, sub, 0:1, :] * alpha
            slope = slope_ref[side, sub, 0:1, :] * alpha
            both = []
            for i, (_, penalty) in enumerate(picked):
                rows = pl.ds(i * BLK, BLK)
                w = jnp.exp2(s_ref[side, sub, rows, :BLK] * (SCALE * LOG2E) - (new + penalty))
                wt = w * s_ref[side, sub, rows, BLK:]
                total = total + jnp.sum(w, axis=0, keepdims=True)
                slope = slope + jnp.sum(wt, axis=0, keepdims=True)
                both.append(
                    jnp.concatenate([w.astype(jnp.bfloat16), wt.astype(jnp.bfloat16)], axis=1)
                )
            values = jnp.concatenate([vt_buf[slot] for slot, _ in picked], axis=1)
            out = jnp.dot(values, jnp.concatenate(both, axis=0), preferred_element_type=jnp.float32)
            m_ref[side, sub, 0:1, :] = new
            sum_ref[side, sub, 0:1, :] = total
            slope_ref[side, sub, 0:1, :] = slope
            acc_ref[side, sub, :HD, :] = acc_ref[side, sub, :HD, :] * alpha + out[:HD, :BLK]
            acc_ref[side, sub, HD:, :] = (
                acc_ref[side, sub, HD:, :] * alpha + out[:HD, BLK:] * SCALE + out[HD:, :BLK]
            )

        if group >= LMAX * count:
            steps = None
        else:
            steps = (jnp.maximum(ends[0][-1], ends[1][-1]) + group - 1) // group
        for sub in range(2):
            if job.fresh:
                m_ref[side, sub] = jnp.full((8, BLK), FLOOR, jnp.float32)
                sum_ref[side, sub] = jnp.zeros((8, BLK), jnp.float32)
                slope_ref[side, sub] = jnp.zeros((8, BLK), jnp.float32)
                acc_ref[side, sub] = jnp.zeros((2 * HD, BLK), jnp.float32)
            else:
                m_ref[side, sub] = state_in[place * 2 + sub, 0:8, :]
                sum_ref[side, sub] = state_in[place * 2 + sub, 8:16, :]
                slope_ref[side, sub] = state_in[place * 2 + sub, 16:24, :]
                acc_ref[side, sub] = state_in[place * 2 + sub, 24:280, :]
        score(0, 0)
        score(1, 0)
        return score, absorb, steps

    def finish(nth):
        place, side = job.places[nth], nth % 2
        for sub in range(2):
            if not job.final:
                state_out[place * 2 + sub, 0:8, :] = m_ref[side, sub]
                state_out[place * 2 + sub, 8:16, :] = sum_ref[side, sub]
                state_out[place * 2 + sub, 16:24, :] = slope_ref[side, sub]
                state_out[place * 2 + sub, 24:280, :] = acc_ref[side, sub]
                continue
            out_ref = out_refs[nth // 2]
            total = sum_ref[side, sub, 0:1, :]
            inv = 1.0 / total
            slope = slope_ref[side, sub, 0:1, :] * (inv * SCALE)
            o = acc_ref[side, sub, :HD, :] * inv
            t = acc_ref[side, sub, HD:, :] * inv - slope * o
            put(out_ref, (place // 4 * 2 + sub) * PART, o, t, m_ref[side, sub, 0:1, :], total, slope)

    ready = prepare(0)
    for nth in range(len(job.places)):
        score, absorb, steps = ready
        last = 0
        if steps is not None:
            last = steps - 1

            def step(n, carry, absorb=absorb, score=score):
                absorb(0, n)
                absorb(1, n)
                score(0, n + 1)
                score(1, n + 1)
                return carry

            lax.fori_loop(0, last, step, 0)
        if nth + 1 < len(job.places):
            ready = prepare(nth + 1)
        absorb(0, last)
        absorb(1, last)
        finish(nth)


def stats_of(ref, base):
    stats = ref[pl.ds(base + 2 * HD, STAT), :].astype(jnp.float32)
    return [stats[3 * i:3 * i + 1] + stats[3 * i + 1:3 * i + 2] + stats[3 * i + 2:3 * i + 3] for i in range(3)]


def weigh(peaks, totals, slopes):
    peak = peaks[0]
    for p in peaks[1:]:
        peak = jnp.maximum(peak, p)
    shares = [l * jnp.exp2(p - peak) for l, p in zip(totals, peaks)]
    total = sum(shares[1:], shares[0])
    inv = 1.0 / total
    shares = [a * inv for a in shares]
    slope = sum((a * s for a, s in zip(shares[1:], slopes[1:])), shares[0] * slopes[0])
    return peak, total, slope, shares


def merge(part_refs, at, sub):
    base = at + sub * PART
    peaks, totals, slopes = zip(*(stats_of(ref, base) for ref in part_refs))
    peak, total, slope, shares = weigh(peaks, totals, slopes)
    o = jnp.zeros((HD, BLK), jnp.float32)
    t = jnp.zeros((HD, BLK), jnp.float32)
    for ref, a, s in zip(part_refs, shares, slopes):
        oj = ref[pl.ds(base, HD), :].astype(jnp.float32)
        tj = ref[pl.ds(base + HD, HD), :].astype(jnp.float32)
        o = o + a * oj
        t = t + a * tj + (a * (s - slope)) * oj
    return o, t, peak, total, slope


def put(out_ref, base, o, t, peak, total, slope):
    rows = split3(peak) + split3(total) + split3(slope)
    rows.append(jnp.zeros((STAT - 9, BLK), jnp.float32))
    out_ref[pl.ds(base, HD), :] = o.astype(jnp.bfloat16)
    out_ref[pl.ds(base + HD, HD), :] = t.astype(jnp.bfloat16)
    out_ref[pl.ds(base + 2 * HD, STAT), :] = jnp.concatenate(rows, axis=0).astype(jnp.bfloat16)


def beyond_kernel(*refs):
    for sub in range(2):
        put(refs[-1], sub * PART, *merge(refs[:-1], 2 * PART, sub))


def within_kernel(*refs):
    part_refs, (o_ref, t_ref, stat_ref) = refs[:-3], refs[-3:]
    for sub in range(2):
        o, t, peak, total, slope = merge(part_refs, 0, sub)
        o_ref[sub] = o
        t_ref[sub] = t
        stat_ref[sub] = jnp.concatenate([peak, total, slope, jnp.zeros((5, BLK), jnp.float32)], axis=0)


def combine_kernel(o_in, t_in, stat_in, part, o_ref, t_ref):
    for sub in range(2):
        base = sub * PART
        first = [stat_in[sub, i:i + 1, :] for i in range(3)]
        second = stats_of(part, base)
        _, _, slope, (a, b) = weigh(*([p, q] for p, q in zip(first, second)))
        oj = part[pl.ds(base, HD), :].astype(jnp.float32)
        tj = part[pl.ds(base + HD, HD), :].astype(jnp.float32)
        o = a * o_in[sub] + b * oj
        t = a * t_in[sub] + b * tj + (a * (first[2] - slope)) * o_in[sub] + (b * (second[2] - slope)) * oj
        o_ref[pl.ds(sub * BLK, BLK), :] = o.T.astype(jnp.bfloat16)
        t_ref[pl.ds(sub * BLK, BLK), :] = t.T.astype(jnp.bfloat16)


def shift(size, k):
    return [(i, (i + k) % size) for i in range(size)]


def attend(job, me, tables, *arrays):
    smem = pl.BlockSpec(memory_space=pltpu.SMEM)
    vmem = pl.BlockSpec(memory_space=pltpu.VMEM)
    anywhere = pl.BlockSpec(memory_space=pl.ANY)
    count, n_shards, n_out = len(job.slabs), 4 * len(job.slabs), len(job.places)
    shape = jax.ShapeDtypeStruct
    k_shape, v_shape = (n_shards * 2 * BLK, 2 * HD), (n_shards * 2, 2 * HD, BLK)
    in_specs = [smem] + [anywhere] * count
    in_specs += [vmem] * 4 if job.fresh else [vmem] * 2
    in_specs += [vmem] * len(job.pieces) if job.pieces else [vmem] * 2
    if job.fresh:
        outs = [shape((16, 2 * HD, 2 * BLK), jnp.bfloat16), shape((16, 24 + 2 * HD, BLK), jnp.float32)]
    else:
        outs = [shape((4 * PART, BLK), jnp.bfloat16)] * (n_out // 2)
    if job.keep:
        outs = outs + [shape(k_shape, jnp.bfloat16), shape(v_shape, jnp.bfloat16)]
    scratch = [
        pltpu.SMEM((count, 16, 128), jnp.int32),
        pltpu.VMEM((2, 2, job.group * BLK, 2 * BLK), jnp.float32),
        pltpu.VMEM((2, 2, 8, BLK), jnp.float32),
        pltpu.VMEM((2, 2, 8, BLK), jnp.float32),
        pltpu.VMEM((2, 2, 8, BLK), jnp.float32),
        pltpu.VMEM((2, 2, 8, BLK), jnp.float32),
        pltpu.VMEM((2, 2, 2 * HD, BLK), jnp.float32),
        pltpu.SemaphoreType.DMA((count,)),
    ]
    if job.pieces and not job.keep:
        scratch += [pltpu.VMEM(k_shape, jnp.bfloat16), pltpu.VMEM(v_shape, jnp.bfloat16)]
    pairs = 2 * n_out * count * 4
    return pl.pallas_call(
        functools.partial(attend_kernel, job),
        out_shape=outs,
        in_specs=in_specs,
        out_specs=[vmem] * len(outs),
        scratch_shapes=scratch,
        compiler_params=pltpu.CompilerParams(vmem_limit_bytes=job.room * 2**20),
        cost_estimate=pl.CostEstimate(
            flops=pairs * 60_000_000, bytes_accessed=4 * 2**20, transcendentals=pairs * BLK * BLK
        ),
        name=job.name,
    )(me, *tables, *arrays)


def shards(q, qt, k, v, kt, vt, block_list, block_count):
    me = jnp.stack([lax.axis_index(a) for a in ("yl", "c", "x", "yh", "z")]).astype(jnp.int32)
    flip = [(0, 1), (1, 0)]
    shard = 4 * TOK

    own = jnp.concatenate([k, kt, v, vt], axis=0)
    own, block_list, block_count = lax.optimization_barrier((own, block_list, block_count))
    beside = lax.ppermute(own, "yl", flip)
    asked = jnp.concatenate([q, qt], axis=0)
    partner = lax.ppermute(asked, "yh", flip)
    table = jnp.concatenate([block_list[:, 0, :], block_count, jnp.zeros((64, 119), jnp.int32)], axis=1)
    tables = [table] + [lax.ppermute(table, "x", shift(NX, d)) for d in (1, 2, 3)]
    pair = jnp.concatenate([own, beside], axis=0)
    asked = jnp.concatenate([asked, partner], axis=0)
    pair, asked, *tables = lax.optimization_barrier((pair, asked, *tables))
    ahead = lax.ppermute(pair, "x", shift(NX, 1))
    behind = lax.ppermute(pair, "x", shift(NX, 3))
    far0 = lax.ppermute(ahead[:shard], "x", shift(NX, 1))
    far1 = lax.ppermute(behind[shard:], "x", shift(NX, 3))
    mine = [pair, ahead, behind]
    theirs = [lax.ppermute(a, "c", flip) for a in mine]

    queries = [asked] + [lax.ppermute(asked, "z", shift(NZ, d)) for d in (1, 2, 3)]

    near = Job("near", (0,), tuple(range(8)), [(0, 2), (2, 2)], True, False, False, GROUP, 12)
    pieces = [((dx - 1) * 4 + dc * 2 + dyl, n) for dc in range(2) for dx, dyl, n in PIECES]
    away = Job("away", (1, 2, 3), (1, 5, 2, 6, 3, 7), pieces, False, True, True, GROUP, 16)
    home = Job("home", (1, 2, 3), (0, 4), [], False, True, False, GROUP, 12)
    wq, state = attend(near, me, tables[:1], *queries, mine[0], theirs[0])
    far0, far1, wq, state = lax.optimization_barrier((far0, far1, wq, state))
    far = [far0, far1]
    mine = mine[1:] + far
    theirs = theirs[1:] + [lax.ppermute(a, "c", flip) for a in far]
    *outer, k_buf, vt_buf = attend(away, me, tables[1:], wq, state, *mine, *theirs)
    inner = attend(home, me, tables[1:], wq, state, k_buf, vt_buf)
    back = list(inner)
    for dz, part in zip((1, 2, 3), outer):
        back.append(lax.ppermute(part, "z", shift(NZ, NZ - dz)))
    theirs = small("beyond", beyond_kernel, [((2 * PART, BLK), jnp.bfloat16)], *back)[0]
    theirs = lax.ppermute(theirs, "yh", flip)
    own = small("within", within_kernel, [((2, n, BLK), jnp.float32) for n in (HD, HD, 8)], *back)
    return tuple(small("combine", combine_kernel, [((TOK, HD), jnp.bfloat16)] * 2, *own, theirs))


def small(name, kernel, outs, *arrays):
    vmem = pl.BlockSpec(memory_space=pltpu.VMEM)
    return pl.pallas_call(
        kernel,
        out_shape=[jax.ShapeDtypeStruct(*out) for out in outs],
        in_specs=[vmem] * len(arrays),
        out_specs=[vmem] * len(outs),
        compiler_params=pltpu.CompilerParams(vmem_limit_bytes=8 * 2**20),
        name=name,
    )(*arrays)


def solution(mesh):
    split = Mesh(np.asarray(mesh.devices).reshape(2, 2, NX, 2, NZ), ("yl", "c", "x", "yh", "z"))
    pb, kv = ("yl", "c"), ("x", "yh", "z")
    row = P(pb + kv, None)
    return jax.shard_map(
        shards,
        mesh=split,
        in_specs=(row,) * 6 + (P(pb, kv, None), P(pb, kv)),
        out_specs=(row, row),
        check_vma=False,
    )
```

time: 91.5 us -> 84.9 us (0.928)
  starting transfers between devices: 37.3 us -> 27.8 us
  waiting for transfers between devices: 22.4 us -> 28.9 us
  local copies, waits for them, and re-layouts: 6.03 us -> 1.71 us
  other arithmetic: 1.91 us -> 2.84 us
    ppermute x9 -> x6, starting transfers between devices: 23.2 us -> 12.1 us  [the longest x3 5.15 us: shards(): back.append(lax.ppermute(part, 'z', shift(NZ, NZ - dz)))]
    ppermute x1, waiting for transfers between devices: 6.77 us -> 0.89 us  [shards(): ahead = lax.ppermute(pair, 'x', shift(NX, 1))]
    unnamed x10 -> x0, local copies, waits for them, and re-layouts: 5.78 us -> none
    ppermute x1, waiting for transfers between devices: 0.01 us -> 5.45 us  [shards(): behind = lax.ppermute(pair, 'x', shift(NX, 3))]
    ppermute x9 -> x6, waiting for transfers between devices: 10.7 us -> 14 us  [the longest x3 9.52 us: shards(): back.append(lax.ppermute(part, 'z', shift(NZ, NZ - dz)))]
    ppermute x3, waiting for transfers between devices: 0.01 us -> 2.53 us  [shards(): lax.ppermute(table, 'x', shift(NX, d))]
    ppermute x1, starting transfers between devices: 0.01 us -> 2.38 us  [shards(): far1 = lax.ppermute(behind[shard:], 'x', shift(NX, 3))]
    ppermute x1, starting transfers between devices: 2.42 us -> 0.41 us  [shards(): behind = lax.ppermute(pair, 'x', shift(NX, 3))]
  transfers between devices with their start and end apart: 24 -> 21, of which waited for: 10 -> 12; matrix products, arithmetic and copies ran while one was open for 7% -> 4% of each run, Pallas kernels for 16% -> 13%
where the time goes in v2:
time: 84.9 us; the launch traced here: 83.6 us
  waiting for transfers between devices  28.9 us (34%)
  starting transfers between devices  27.8 us (33%)
  Pallas kernels  21.5 us (25%)
  other arithmetic  2.84 us (3%)
  local copies, waits for them, and re-layouts  1.71 us (2%)
    pallas_call x3, Pallas kernels, attend(): pl.pallas_call(functools.partial(attend_kernel, job), out_shape=outs, in_...  20.3 us
    ppermute x3, waiting for transfers between devices, shards(): back.append(lax.ppermute(part, 'z', shift(NZ, NZ - dz)))  9.52 us
    ppermute x3, starting transfers between devices, shards(): lax.ppermute(asked, 'z', shift(NZ, d))  5.96 us
    ppermute x1, waiting for transfers between devices, shards(): behind = lax.ppermute(pair, 'x', shift(NX, 3))  5.45 us
    ppermute x3, starting transfers between devices, shards(): back.append(lax.ppermute(part, 'z', shift(NZ, NZ - dz)))  5.15 us
    ppermute x3, waiting for transfers between devices, shards(): lax.ppermute(asked, 'z', shift(NZ, d))  4.78 us
    ppermute x3, starting transfers between devices, shards(): lax.ppermute(table, 'x', shift(NX, d))  4.45 us
    ppermute x1, waiting for transfers between devices, shards(): theirs = lax.ppermute(theirs, 'yh', flip)  3.73 us
  transfers between devices with their start and end apart: 21, of which 12 were waited for; matrix products, arithmetic and copies ran while one was open for 4% of the time, Pallas kernels for 13%

profile of v2, /device:TPU:0, one launch (start us, length us, event | category | flops | bytes accessed | tf_op | source)
XLA Modules:
  0.0 83.6 jit_solution(16182939410814367801)
XLA Ops:
  0.6 0.9 %pad_maximum_fusion.3 = bf16[512,128]{1,0:T(8,128)(2,1)S(1)} fusion(bf16[256,128]{1,0:T(8,128)(2,1)} %param.9, bf16[256,128]{1,0:T(8,128)(2,1)} %param.8), kind=kLoop, calls=%fused_computation.3 | loop fusion | flops 262144 | bytes 262144 | tf_op jit(solution)/shard_map/concatenate | solution.py:342
  1.5 3.4 %collective-permute-start.1 = (bf16[512,128]{1,0:T(8,128)(2,1)S(1)}, bf16[512,128]{1,0:T(8,128)(2,1)S(1)}, u32[]{:S(2)}, u32[]{:S(2)}) collective-permute-start(bf16[512,128]{1,0:T(8,128)(2,1)S(1)} %pad_maximum_fusion.3), channel_id=1, source_target_pairs={{0,4},{4,0},{1,5},{5,1},{2,6},{6,2},{3,7},{7,3},{8,12},{12,8},{9,1... | collective-permute-start | bytes 393224 | tf_op jit(solution)/shard_map/ppermute | solution.py:343
  4.9 1.0 %pad_maximum_fusion.1 = bf16[1024,128]{1,0:T(8,128)(2,1)S(1)} fusion(bf16[256,128]{1,0:T(8,128)(2,1)} %param.13, bf16[256,128]{1,0:T(8,128)(2,1)} %param.11, bf16[256,128]{1,0:T(8,128)(2,1)} %param.12, bf16[256,128]{1,0:T(8,128)(2,1)} %param.10), kind=kLoop, calls=%fused_computation.1 | loop fusion | flops 1048576 | bytes 524288 | tf_op jit(solution)/shard_map/concatenate | solution.py:339
  8.3 2.8 %collective-permute-start.4 = (s32[64,128]{1,0:T(8,128)S(1)}, s32[64,128]{1,0:T(8,128)S(1)}, u32[]{:S(2)}, u32[]{:S(2)}) collective-permute-start(s32[64,128]{1,0:T(8,128)S(1)} %add_add_fusion.refs_0_), channel_id=1, source_target_pairs={{0,24},{8,0},{16,8},{24,16},{1,25},{9,1},{17,9},{25,17},{2,26},{10... | collective-permute-start | bytes 98312 | tf_op jit(solution)/shard_map/ppermute | solution.py:345
  11.8 0.9 %collective-permute-start.2 = (s32[64,128]{1,0:T(8,128)S(1)}, s32[64,128]{1,0:T(8,128)S(1)}, u32[]{:S(2)}, u32[]{:S(2)}) collective-permute-start(s32[64,128]{1,0:T(8,128)S(1)} %add_add_fusion.refs_0_), channel_id=1, source_target_pairs={{0,8},{8,16},{16,24},{24,0},{1,9},{9,17},{17,25},{25,1},{2,10},{10... | collective-permute-start | bytes 98312 | tf_op jit(solution)/shard_map/ppermute | solution.py:345
  12.7 0.9 %pad_maximum_fusion.2.refs_1_ = bf16[1024,128]{1,0:T(8,128)(2,1)S(1)} fusion(bf16[512,128]{1,0:T(8,128)(2,1)S(1)} %collective-permute-done.1, bf16[256,128]{1,0:T(8,128)(2,1)} %param.9, bf16[256,128]{1,0:T(8,128)(2,1)} %param.8), kind=kLoop, calls=%fused_computation.2 | loop fusion | flops 786432 | bytes 524288 | tf_op jit(solution)/shard_map/concatenate | solution.py:347
  14.4 2.0 %collective-permute-done.3.refs_1_ = s32[64,128]{1,0:T(8,128)S(1)} collective-permute-done((s32[64,128]{1,0:T(8,128)S(1)}, s32[64,128]{1,0:T(8,128)S(1)}, u32[]{:S(2)}, u32[]{:S(2)}) %collective-permute-start.3) | collective-permute-done | bytes 32800 | tf_op jit(solution)/shard_map/ppermute | solution.py:345
  17.4 1.6 %collective-permute-start.5 = (bf16[2048,128]{1,0:T(8,128)(2,1)S(1)}, bf16[2048,128]{1,0:T(8,128)(2,1)S(1)}, u32[]{:S(2)}, u32[]{:S(2)}) collective-permute-start(bf16[2048,128]{1,0:T(8,128)(2,1)S(1)} %pad_maximum_fusion.refs_5_), channel_id=1, source_target_pairs={{0,8},{8,16},{16,24},{24,0},{1,9},{9,17},{17,25},{25,1},{2,10},{10... | collective-permute-start | bytes 1572872 | tf_op jit(solution)/shard_map/ppermute | solution.py:349
  19.0 4.0 %collective-permute-start.11 = (bf16[1024,128]{1,0:T(8,128)(2,1)S(1)}, bf16[1024,128]{1,0:T(8,128)(2,1)S(1)}, u32[]{:S(2)}, u32[]{:S(2)}) collective-permute-start(bf16[1024,128]{1,0:T(8,128)(2,1)S(1)} %pad_maximum_fusion.2.refs_1_), channel_id=1, source_target_pairs={{0,3},{1,0},{2,1},{3,2},{4,7},{5,4},{6,5},{7,6},{8,11},{9,8},{10,9... | collective-permute-start | bytes 786440 | tf_op jit(solution)/shard_map/ppermute | solution.py:356
  23.0 5.4 %collective-permute-done.7.refs_6_ = bf16[2048,128]{1,0:T(8,128)(2,1)S(1)} collective-permute-done((bf16[2048,128]{1,0:T(8,128)(2,1)S(1)}, bf16[2048,128]{1,0:T(8,128)(2,1)S(1)}, u32[]{:S(2)}, u32[]{:S(2)}) %collective-permute-start.7) | collective-permute-done | bytes 524320 | tf_op jit(solution)/shard_map/ppermute | solution.py:350
  28.5 1.9 %collective-permute-start.9 = (bf16[1024,128]{1,0:T(8,128)(2,1)S(1)}, bf16[1024,128]{1,0:T(8,128)(2,1)S(1)}, u32[]{:S(2)}, u32[]{:S(2)}) collective-permute-start(bf16[1024,128]{1,0:T(8,128)(2,1)S(1)} %pad_maximum_fusion.2.refs_1_), channel_id=1, source_target_pairs={{0,1},{1,2},{2,3},{3,0},{4,5},{5,6},{6,7},{7,4},{8,9},{9,10},{10,1... | collective-permute-start | bytes 786440 | tf_op jit(solution)/shard_map/ppermute | solution.py:356
  30.5 0.9 %collective-permute-done.5.refs_5_ = bf16[2048,128]{1,0:T(8,128)(2,1)S(1)} collective-permute-done((bf16[2048,128]{1,0:T(8,128)(2,1)S(1)}, bf16[2048,128]{1,0:T(8,128)(2,1)S(1)}, u32[]{:S(2)}, u32[]{:S(2)}) %collective-permute-start.5) | collective-permute-done | bytes 524320 | tf_op jit(solution)/shard_map/ppermute | solution.py:349
  31.4 2.4 %collective-permute-start.8 = (bf16[1024,128]{1,0:T(8,128)(2,1)S(1)}, bf16[1024,128]{1,0:T(8,128)(2,1)S(1)}, u32[]{:S(2)}, u32[]{:S(2)}) collective-permute-start(bf16[1024,128]{1,0:T(8,128)(2,1)S(1)} %slice.9), channel_id=1, source_target_pairs={{0,24},{8,0},{16,8},{24,16},{1,25},{9,1},{17,9},{25,17},{2,26},{10... | collective-permute-start | bytes 786440 | tf_op jit(solution)/shard_map/ppermute | solution.py:352
  33.8 1.1 %collective-permute-done.11.refs_4_ = bf16[1024,128]{1,0:T(8,128)(2,1)S(1)} collective-permute-done((bf16[1024,128]{1,0:T(8,128)(2,1)S(1)}, bf16[1024,128]{1,0:T(8,128)(2,1)S(1)}, u32[]{:S(2)}, u32[]{:S(2)}) %collective-permute-start.11) | collective-permute-done | bytes 262176 | tf_op jit(solution)/shard_map/ppermute | solution.py:356
  34.9 3.7 %collective-permute-done.9.refs_2_ = bf16[1024,128]{1,0:T(8,128)(2,1)S(1)} collective-permute-done((bf16[1024,128]{1,0:T(8,128)(2,1)S(1)}, bf16[1024,128]{1,0:T(8,128)(2,1)S(1)}, u32[]{:S(2)}, u32[]{:S(2)}) %collective-permute-start.9) | collective-permute-done | bytes 262176 | tf_op jit(solution)/shard_map/ppermute | solution.py:356
  38.6 6.5 %near.1 = (bf16[16,256,256]{2,1,0:T(8,128)(2,1)S(1)}, f32[16,280,128]{2,1,0:T(8,128)S(1)}) custom-call(s32[5]{0:T(128)S(1)} %stack.23.me_ref, s32[64,128]{1,0:T(8,128)S(1)} %add_add_fusion.refs_0_, bf16[1024,128]{1,0:T(8,128)(2,1)S(1)} %pad_maximum_fusion.2.refs_1_, bf16[1024,128]{1,0:T(8,128)(2,1)S(1)} %collective-permute-done.9.refs_2_, ...), custom_call_target="tpu_custom_call" | custom-call | flops 3840000000 | bytes 4194304 | tf_op jit(solution)/shard_map/near/pallas_call | solution.py:320
  47.2 9.6 %away.1 = (bf16[1088,128]{1,0:T(8,128)(2,1)S(1)}, bf16[1088,128]{1,0:T(8,128)(2,1)S(1)}, bf16[1088,128]{1,0:T(8,128)(2,1)S(1)}, bf16[3072,256]{1,0:T(8,128)(2,1)S(1)}, bf16[24,256,128]{2,1,0:T(8,128)(2,1)S(1)}) custom-call(s32[5]{0:T(128)S(1)} %stack.23.me_ref, s32[64,128]{1,0:T(8,128)S(1)} %collective-permute-done.2.refs_0_, ...), custom_call_target="tpu_custom_call" | custom-call | flops 8640000000 | bytes 4194304 | tf_op jit(solution)/shard_map/away/pallas_call | solution.py:320
  56.8 4.2 %collective-permute-start.17 = (bf16[1088,128]{1,0:T(8,128)(2,1)S(1)}, bf16[1088,128]{1,0:T(8,128)(2,1)S(1)}, u32[]{:S(2)}, u32[]{:S(2)}) collective-permute-start(bf16[1088,128]{1,0:T(8,128)(2,1)S(1)} %get-tuple-element.42), channel_id=1, source_target_pairs={{0,3},{1,0},{2,1},{3,2},{4,7},{5,4},{6,5},{7,6},{8,11},{9,8},{10,9... | collective-permute-start | bytes 835592 | tf_op jit(solution)/shard_map/ppermute | solution.py:371
  61.0 0.9 %collective-permute-start.19 = (bf16[1088,128]{1,0:T(8,128)(2,1)S(1)}, bf16[1088,128]{1,0:T(8,128)(2,1)S(1)}, u32[]{:S(2)}, u32[]{:S(2)}) collective-permute-start(bf16[1088,128]{1,0:T(8,128)(2,1)S(1)} %get-tuple-element.44), channel_id=1, source_target_pairs={{0,1},{1,2},{2,3},{3,0},{4,5},{5,6},{6,7},{7,4},{8,9},{9,10},{10,1... | collective-permute-start | bytes 835592 | tf_op jit(solution)/shard_map/ppermute | solution.py:371
  61.9 4.3 %home.1.refs_0_ = bf16[1088,128]{1,0:T(8,128)(2,1)S(1)} custom-call(s32[5]{0:T(128)S(1)} %stack.23.me_ref, s32[64,128]{1,0:T(8,128)S(1)} %collective-permute-done.2.refs_0_, s32[64,128]{1,0:T(8,128)S(1)} %collective-permute-done.3.refs_1_, s32[64,128]{1,0:T(8,128)S(1)} %collective-permute-done.4.refs_2_, ...), custom_call_target="tpu_custom_call" | custom-call | flops 2880000000 | bytes 4194304 | tf_op jit(solution)/shard_map/home/pallas_call | solution.py:320
  66.2 6.1 %collective-permute-done.17.refs_1_ = bf16[1088,128]{1,0:T(8,128)(2,1)S(1)} collective-permute-done((bf16[1088,128]{1,0:T(8,128)(2,1)S(1)}, bf16[1088,128]{1,0:T(8,128)(2,1)S(1)}, u32[]{:S(2)}, u32[]{:S(2)}) %collective-permute-start.17) | collective-permute-done | bytes 278560 | tf_op jit(solution)/shard_map/ppermute | solution.py:371
  72.3 3.4 %collective-permute-done.19.refs_3_ = bf16[1088,128]{1,0:T(8,128)(2,1)S(1)} collective-permute-done((bf16[1088,128]{1,0:T(8,128)(2,1)S(1)}, bf16[1088,128]{1,0:T(8,128)(2,1)S(1)}, u32[]{:S(2)}, u32[]{:S(2)}) %collective-permute-start.19) | collective-permute-done | bytes 278560 | tf_op jit(solution)/shard_map/ppermute | solution.py:371
  75.9 2.9 %collective-permute-start.20 = (bf16[544,128]{1,0:T(8,128)(2,1)S(1)}, bf16[544,128]{1,0:T(8,128)(2,1)S(1)}, u32[]{:S(2)}, u32[]{:S(2)}) collective-permute-start(bf16[544,128]{1,0:T(8,128)(2,1)S(1)} %beyond.1), channel_id=1, source_target_pairs={{0,4},{4,0},{1,5},{5,1},{2,6},{6,2},{3,7},{7,3},{8,12},{12,8},{9,1... | collective-permute-start | bytes 417800 | tf_op jit(solution)/shard_map/ppermute | solution.py:373
  79.0 3.7 %collective-permute-done.20.part = bf16[544,128]{1,0:T(8,128)(2,1)S(1)} collective-permute-done((bf16[544,128]{1,0:T(8,128)(2,1)S(1)}, bf16[544,128]{1,0:T(8,128)(2,1)S(1)}, u32[]{:S(2)}, u32[]{:S(2)}) %collective-permute-start.20) | collective-permute-done | bytes 139296 | tf_op jit(solution)/shard_map/ppermute | solution.py:373
  (36 shorter events, 8.4 us)
Async XLA Ops:
  1.5 11.2 %collective-permute-start.1 = (bf16[512,128]{1,0:T(8,128)(2,1)S(1)}, bf16[512,128]{1,0:T(8,128)(2,1)S(1)}, u32[]{:S(2)}, u32[]{:S(2)}) collective-permute-start(bf16[512,128]{1,0:T(8,128)(2,1)S(1)} %pad_maximum_fusion.3), channel_id=1, source_target_pairs={{0,4},{4,0},{1,5},{5,1},{2,6},{6,2},{3,7},{7,3},{8,12},{12,8},{9,1... | collective-permute-start | bytes 393224 | tf_op jit(solution)/shard_map/ppermute | solution.py:343
  5.8 8.6 %collective-permute-start = (bf16[1024,128]{1,0:T(8,128)(2,1)S(1)}, bf16[1024,128]{1,0:T(8,128)(2,1)S(1)}, u32[]{:S(2)}, u32[]{:S(2)}) collective-permute-start(bf16[1024,128]{1,0:T(8,128)(2,1)S(1)} %pad_maximum_fusion.1), channel_id=1, source_target_pairs={{0,64},{64,0},{1,65},{65,1},{2,66},{66,2},{3,67},{67,3},{4,68},{68... | collective-permute-start | bytes 786440 | tf_op jit(solution)/shard_map/ppermute | solution.py:341
  8.3 6.2 %collective-permute-start.4 = (s32[64,128]{1,0:T(8,128)S(1)}, s32[64,128]{1,0:T(8,128)S(1)}, u32[]{:S(2)}, u32[]{:S(2)}) collective-permute-start(s32[64,128]{1,0:T(8,128)S(1)} %add_add_fusion.refs_0_), channel_id=1, source_target_pairs={{0,24},{8,0},{16,8},{24,16},{1,25},{9,1},{17,9},{25,17},{2,26},{10... | collective-permute-start | bytes 98312 | tf_op jit(solution)/shard_map/ppermute | solution.py:345
  11.0 5.4 %collective-permute-start.3 = (s32[64,128]{1,0:T(8,128)S(1)}, s32[64,128]{1,0:T(8,128)S(1)}, u32[]{:S(2)}, u32[]{:S(2)}) collective-permute-start(s32[64,128]{1,0:T(8,128)S(1)} %add_add_fusion.refs_0_), channel_id=1, source_target_pairs={{0,16},{8,24},{16,0},{24,8},{1,17},{9,25},{17,1},{25,9},{2,18},{10... | collective-permute-start | bytes 98312 | tf_op jit(solution)/shard_map/ppermute | solution.py:345
  11.8 5.1 %collective-permute-start.2 = (s32[64,128]{1,0:T(8,128)S(1)}, s32[64,128]{1,0:T(8,128)S(1)}, u32[]{:S(2)}, u32[]{:S(2)}) collective-permute-start(s32[64,128]{1,0:T(8,128)S(1)} %add_add_fusion.refs_0_), channel_id=1, source_target_pairs={{0,8},{8,16},{16,24},{24,0},{1,9},{9,17},{17,25},{25,1},{2,10},{10... | collective-permute-start | bytes 98312 | tf_op jit(solution)/shard_map/ppermute | solution.py:345
  17.0 11.5 %collective-permute-start.7 = (bf16[2048,128]{1,0:T(8,128)(2,1)S(1)}, bf16[2048,128]{1,0:T(8,128)(2,1)S(1)}, u32[]{:S(2)}, u32[]{:S(2)}) collective-permute-start(bf16[2048,128]{1,0:T(8,128)(2,1)S(1)} %pad_maximum_fusion.refs_5_), channel_id=1, source_target_pairs={{0,24},{8,0},{16,8},{24,16},{1,25},{9,1},{17,9},{25,17},{2,26},{10... | collective-permute-start | bytes 1572872 | tf_op jit(solution)/shard_map/ppermute | solution.py:350
  17.4 14.0 %collective-permute-start.5 = (bf16[2048,128]{1,0:T(8,128)(2,1)S(1)}, bf16[2048,128]{1,0:T(8,128)(2,1)S(1)}, u32[]{:S(2)}, u32[]{:S(2)}) collective-permute-start(bf16[2048,128]{1,0:T(8,128)(2,1)S(1)} %pad_maximum_fusion.refs_5_), channel_id=1, source_target_pairs={{0,8},{8,16},{16,24},{24,0},{1,9},{9,17},{17,25},{25,1},{2,10},{10... | collective-permute-start | bytes 1572872 | tf_op jit(solution)/shard_map/ppermute | solution.py:349
  19.0 19.6 %collective-permute-start.12 = (bf16[2048,128]{1,0:T(8,128)(2,1)S(1)}, bf16[2048,128]{1,0:T(8,128)(2,1)S(1)}, u32[]{:S(2)}, u32[]{:S(2)}) collective-permute-start(bf16[2048,128]{1,0:T(8,128)(2,1)S(1)} %pad_maximum_fusion.refs_5_), channel_id=1, source_target_pairs={{0,32},{32,0},{1,33},{33,1},{2,34},{34,2},{3,35},{35,3},{4,36},{36... | collective-permute-start | bytes 1572872 | tf_op jit(solution)/shard_map/ppermute | solution.py:354
  19.0 15.9 %collective-permute-start.11 = (bf16[1024,128]{1,0:T(8,128)(2,1)S(1)}, bf16[1024,128]{1,0:T(8,128)(2,1)S(1)}, u32[]{:S(2)}, u32[]{:S(2)}) collective-permute-start(bf16[1024,128]{1,0:T(8,128)(2,1)S(1)} %pad_maximum_fusion.2.refs_1_), channel_id=1, source_target_pairs={{0,3},{1,0},{2,1},{3,2},{4,7},{5,4},{6,5},{7,6},{8,11},{9,8},{10,9... | collective-permute-start | bytes 786440 | tf_op jit(solution)/shard_map/ppermute | solution.py:356
  23.0 11.9 %collective-permute-start.10 = (bf16[1024,128]{1,0:T(8,128)(2,1)S(1)}, bf16[1024,128]{1,0:T(8,128)(2,1)S(1)}, u32[]{:S(2)}, u32[]{:S(2)}) collective-permute-start(bf16[1024,128]{1,0:T(8,128)(2,1)S(1)} %pad_maximum_fusion.2.refs_1_), channel_id=1, source_target_pairs={{0,2},{1,3},{2,0},{3,1},{4,6},{5,7},{6,4},{7,5},{8,10},{9,11},{10,... | collective-permute-start | bytes 786440 | tf_op jit(solution)/shard_map/ppermute | solution.py:356
  28.5 10.1 %collective-permute-start.9 = (bf16[1024,128]{1,0:T(8,128)(2,1)S(1)}, bf16[1024,128]{1,0:T(8,128)(2,1)S(1)}, u32[]{:S(2)}, u32[]{:S(2)}) collective-permute-start(bf16[1024,128]{1,0:T(8,128)(2,1)S(1)} %pad_maximum_fusion.2.refs_1_), channel_id=1, source_target_pairs={{0,1},{1,2},{2,3},{3,0},{4,5},{5,6},{6,7},{7,4},{8,9},{9,10},{10,1... | collective-permute-start | bytes 786440 | tf_op jit(solution)/shard_map/ppermute | solution.py:356
  31.4 13.7 %collective-permute-start.8 = (bf16[1024,128]{1,0:T(8,128)(2,1)S(1)}, bf16[1024,128]{1,0:T(8,128)(2,1)S(1)}, u32[]{:S(2)}, u32[]{:S(2)}) collective-permute-start(bf16[1024,128]{1,0:T(8,128)(2,1)S(1)} %slice.9), channel_id=1, source_target_pairs={{0,24},{8,0},{16,8},{24,16},{1,25},{9,1},{17,9},{25,17},{2,26},{10... | collective-permute-start | bytes 786440 | tf_op jit(solution)/shard_map/ppermute | solution.py:352
  34.9 10.2 %collective-permute-start.6 = (bf16[1024,128]{1,0:T(8,128)(2,1)S(1)}, bf16[1024,128]{1,0:T(8,128)(2,1)S(1)}, u32[]{:S(2)}, u32[]{:S(2)}) collective-permute-start(bf16[1024,128]{1,0:T(8,128)(2,1)S(1)} %slice.8), channel_id=1, source_target_pairs={{0,8},{8,16},{16,24},{24,0},{1,9},{9,17},{17,25},{25,1},{2,10},{10... | collective-permute-start | bytes 786440 | tf_op jit(solution)/shard_map/ppermute | solution.py:351
  34.9 11.1 %collective-permute-start.14 = (bf16[2048,128]{1,0:T(8,128)(2,1)S(1)}, bf16[2048,128]{1,0:T(8,128)(2,1)S(1)}, u32[]{:S(2)}, u32[]{:S(2)}) collective-permute-start(bf16[2048,128]{1,0:T(8,128)(2,1)S(1)} %collective-permute-done.7.refs_6_), channel_id=1, source_target_pairs={{0,32},{32,0},{1,33},{33,1},{2,34},{34,2},{3,35},{35,3},{4,36},{36... | collective-permute-start | bytes 1572872 | tf_op jit(solution)/shard_map/ppermute | solution.py:354
  38.6 7.4 %collective-permute-start.13 = (bf16[2048,128]{1,0:T(8,128)(2,1)S(1)}, bf16[2048,128]{1,0:T(8,128)(2,1)S(1)}, u32[]{:S(2)}, u32[]{:S(2)}) collective-permute-start(bf16[2048,128]{1,0:T(8,128)(2,1)S(1)} %collective-permute-done.5.refs_5_), channel_id=1, source_target_pairs={{0,32},{32,0},{1,33},{33,1},{2,34},{34,2},{3,35},{35,3},{4,36},{36... | collective-permute-start | bytes 1572872 | tf_op jit(solution)/shard_map/ppermute | solution.py:354
  45.1 1.7 %collective-permute-start.15 = (bf16[1024,128]{1,0:T(8,128)(2,1)S(1)}, bf16[1024,128]{1,0:T(8,128)(2,1)S(1)}, u32[]{:S(2)}, u32[]{:S(2)}) collective-permute-start(bf16[1024,128]{1,0:T(8,128)(2,1)S(1)} %collective-permute-done.6.refs_7_), channel_id=1, source_target_pairs={{0,32},{32,0},{1,33},{33,1},{2,34},{34,2},{3,35},{35,3},{4,36},{36... | collective-permute-start | bytes 786440 | tf_op jit(solution)/shard_map/ppermute | solution.py:366
  45.7 1.5 %collective-permute-start.16 = (bf16[1024,128]{1,0:T(8,128)(2,1)S(1)}, bf16[1024,128]{1,0:T(8,128)(2,1)S(1)}, u32[]{:S(2)}, u32[]{:S(2)}) collective-permute-start(bf16[1024,128]{1,0:T(8,128)(2,1)S(1)} %collective-permute-done.8.refs_8_), channel_id=1, source_target_pairs={{0,32},{32,0},{1,33},{33,1},{2,34},{34,2},{3,35},{35,3},{4,36},{36... | collective-permute-start | bytes 786440 | tf_op jit(solution)/shard_map/ppermute | solution.py:366
  56.8 15.5 %collective-permute-start.17 = (bf16[1088,128]{1,0:T(8,128)(2,1)S(1)}, bf16[1088,128]{1,0:T(8,128)(2,1)S(1)}, u32[]{:S(2)}, u32[]{:S(2)}) collective-permute-start(bf16[1088,128]{1,0:T(8,128)(2,1)S(1)} %get-tuple-element.42), channel_id=1, source_target_pairs={{0,3},{1,0},{2,1},{3,2},{4,7},{5,4},{6,5},{7,6},{8,11},{9,8},{10,9... | collective-permute-start | bytes 835592 | tf_op jit(solution)/shard_map/ppermute | solution.py:371
  61.0 11.3 %collective-permute-start.18 = (bf16[1088,128]{1,0:T(8,128)(2,1)S(1)}, bf16[1088,128]{1,0:T(8,128)(2,1)S(1)}, u32[]{:S(2)}, u32[]{:S(2)}) collective-permute-start(bf16[1088,128]{1,0:T(8,128)(2,1)S(1)} %get-tuple-element.43), channel_id=1, source_target_pairs={{0,2},{1,3},{2,0},{3,1},{4,6},{5,7},{6,4},{7,5},{8,10},{9,11},{10,... | collective-permute-start | bytes 835592 | tf_op jit(solution)/shard_map/ppermute | solution.py:371
  61.0 14.7 %collective-permute-start.19 = (bf16[1088,128]{1,0:T(8,128)(2,1)S(1)}, bf16[1088,128]{1,0:T(8,128)(2,1)S(1)}, u32[]{:S(2)}, u32[]{:S(2)}) collective-permute-start(bf16[1088,128]{1,0:T(8,128)(2,1)S(1)} %get-tuple-element.44), channel_id=1, source_target_pairs={{0,1},{1,2},{2,3},{3,0},{4,5},{5,6},{6,7},{7,4},{8,9},{9,10},{10,1... | collective-permute-start | bytes 835592 | tf_op jit(solution)/shard_map/ppermute | solution.py:371
  75.9 6.8 %collective-permute-start.20 = (bf16[544,128]{1,0:T(8,128)(2,1)S(1)}, bf16[544,128]{1,0:T(8,128)(2,1)S(1)}, u32[]{:S(2)}, u32[]{:S(2)}) collective-permute-start(bf16[544,128]{1,0:T(8,128)(2,1)S(1)} %beyond.1), channel_id=1, source_target_pairs={{0,4},{4,0},{1,5},{5,1},{2,6},{6,2},{3,7},{7,3},{8,12},{12,8},{9,1... | collective-permute-start | bytes 417800 | tf_op jit(solution)/shard_map/ppermute | solution.py:373

commit v3 on v2

--- a/solution.py
+++ b/solution.py
@@ -357,7 +357,7 @@
 
     near = Job("near", (0,), tuple(range(8)), [(0, 2), (2, 2)], True, False, False, GROUP, 12)
     pieces = [((dx - 1) * 4 + dc * 2 + dyl, n) for dc in range(2) for dx, dyl, n in PIECES]
-    away = Job("away", (1, 2, 3), (1, 5, 2, 6, 3, 7), pieces, False, True, True, GROUP, 16)
+    away = Job("away", (1, 2, 3), (2, 6, 1, 5, 3, 7), pieces, False, True, True, GROUP, 16)
     home = Job("home", (1, 2, 3), (0, 4), [], False, True, False, GROUP, 12)
     wq, state = attend(near, me, tables[:1], *queries, mine[0], theirs[0])
     far0, far1, wq, state = lax.optimization_barrier((far0, far1, wq, state))
@@ -367,7 +367,7 @@
     *outer, k_buf, vt_buf = attend(away, me, tables[1:], wq, state, *mine, *theirs)
     inner = attend(home, me, tables[1:], wq, state, k_buf, vt_buf)
     back = list(inner)
-    for dz, part in zip((1, 2, 3), outer):
+    for dz, part in zip((2, 1, 3), outer):
         back.append(lax.ppermute(part, "z", shift(NZ, NZ - dz)))
     theirs = small("beyond", beyond_kernel, [((2 * PART, BLK), jnp.bfloat16)], *back)[0]
     theirs = lax.ppermute(theirs, "yh", flip)

time: 84.9 us -> 83.5 us (0.984)
  waiting for transfers between devices: 28.9 us -> 25.8 us
  starting transfers between devices: 27.8 us -> 29.1 us
  Pallas kernels: 21.5 us -> 22.4 us
    ppermute x3, waiting for transfers between devices: 9.52 us -> 6.46 us  [shards(): back.append(lax.ppermute(part, 'z', shift(NZ, NZ - dz)))]
    ppermute x1, starting transfers between devices: 2.88 us -> 5.14 us  [shards(): theirs = lax.ppermute(theirs, 'yh', flip)]
    ppermute x3, starting transfers between devices: 5.15 us -> 4.21 us  [shards(): back.append(lax.ppermute(part, 'z', shift(NZ, NZ - dz)))]
  transfers between devices with their start and end apart: 21 -> 21, of which waited for: 12 -> 13; matrix products, arithmetic and copies ran while one was open for 4% -> 4% of each run, Pallas kernels for 13% -> 12%
where the time goes in v3:
time: 83.5 us; the launch traced here: 82.6 us
  starting transfers between devices  29.1 us (35%)
  waiting for transfers between devices  25.8 us (31%)
  Pallas kernels  22.4 us (27%)
  other arithmetic  2.84 us (3%)
  local copies, waits for them, and re-layouts  1.71 us (2%)
    pallas_call x3, Pallas kernels, attend(): pl.pallas_call(functools.partial(attend_kernel, job), out_shape=outs, in_...  21.1 us
    ppermute x3, waiting for transfers between devices, shards(): back.append(lax.ppermute(part, 'z', shift(NZ, NZ - dz)))  6.46 us
    ppermute x3, starting transfers between devices, shards(): lax.ppermute(asked, 'z', shift(NZ, d))  5.96 us
    ppermute x1, waiting for transfers between devices, shards(): behind = lax.ppermute(pair, 'x', shift(NX, 3))  5.45 us
    ppermute x1, starting transfers between devices, shards(): theirs = lax.ppermute(theirs, 'yh', flip)  5.14 us
    ppermute x3, waiting for transfers between devices, shards(): lax.ppermute(asked, 'z', shift(NZ, d))  4.78 us
    ppermute x3, starting transfers between devices, shards(): lax.ppermute(table, 'x', shift(NX, d))  4.45 us
    ppermute x3, starting transfers between devices, shards(): back.append(lax.ppermute(part, 'z', shift(NZ, NZ - dz)))  4.21 us
  transfers between devices with their start and end apart: 21, of which 13 were waited for; matrix products, arithmetic and copies ran while one was open for 4% of the time, Pallas kernels for 12%

profile of v3, /device:TPU:0, one launch (start us, length us, event | category | flops | bytes accessed | tf_op | source)
XLA Modules:
  0.0 82.6 jit_solution(11854164210107620693)
XLA Ops:
  0.6 0.9 %pad_maximum_fusion.3 = bf16[512,128]{1,0:T(8,128)(2,1)S(1)} fusion(bf16[256,128]{1,0:T(8,128)(2,1)} %param.9, bf16[256,128]{1,0:T(8,128)(2,1)} %param.8), kind=kLoop, calls=%fused_computation.3 | loop fusion | flops 262144 | bytes 262144 | tf_op jit(solution)/shard_map/concatenate | solution.py:342
  1.5 3.4 %collective-permute-start.1 = (bf16[512,128]{1,0:T(8,128)(2,1)S(1)}, bf16[512,128]{1,0:T(8,128)(2,1)S(1)}, u32[]{:S(2)}, u32[]{:S(2)}) collective-permute-start(bf16[512,128]{1,0:T(8,128)(2,1)S(1)} %pad_maximum_fusion.3), channel_id=1, source_target_pairs={{0,4},{4,0},{1,5},{5,1},{2,6},{6,2},{3,7},{7,3},{8,12},{12,8},{9,1... | collective-permute-start | bytes 393224 | tf_op jit(solution)/shard_map/ppermute | solution.py:343
  4.9 1.0 %pad_maximum_fusion.1 = bf16[1024,128]{1,0:T(8,128)(2,1)S(1)} fusion(bf16[256,128]{1,0:T(8,128)(2,1)} %param.13, bf16[256,128]{1,0:T(8,128)(2,1)} %param.11, bf16[256,128]{1,0:T(8,128)(2,1)} %param.12, bf16[256,128]{1,0:T(8,128)(2,1)} %param.10), kind=kLoop, calls=%fused_computation.1 | loop fusion | flops 1048576 | bytes 524288 | tf_op jit(solution)/shard_map/concatenate | solution.py:339
  8.3 2.8 %collective-permute-start.4 = (s32[64,128]{1,0:T(8,128)S(1)}, s32[64,128]{1,0:T(8,128)S(1)}, u32[]{:S(2)}, u32[]{:S(2)}) collective-permute-start(s32[64,128]{1,0:T(8,128)S(1)} %add_add_fusion.refs_0_), channel_id=1, source_target_pairs={{0,24},{8,0},{16,8},{24,16},{1,25},{9,1},{17,9},{25,17},{2,26},{10... | collective-permute-start | bytes 98312 | tf_op jit(solution)/shard_map/ppermute | solution.py:345
  11.8 0.9 %collective-permute-start.2 = (s32[64,128]{1,0:T(8,128)S(1)}, s32[64,128]{1,0:T(8,128)S(1)}, u32[]{:S(2)}, u32[]{:S(2)}) collective-permute-start(s32[64,128]{1,0:T(8,128)S(1)} %add_add_fusion.refs_0_), channel_id=1, source_target_pairs={{0,8},{8,16},{16,24},{24,0},{1,9},{9,17},{17,25},{25,1},{2,10},{10... | collective-permute-start | bytes 98312 | tf_op jit(solution)/shard_map/ppermute | solution.py:345
  12.7 0.9 %pad_maximum_fusion.2.refs_1_ = bf16[1024,128]{1,0:T(8,128)(2,1)S(1)} fusion(bf16[512,128]{1,0:T(8,128)(2,1)S(1)} %collective-permute-done.1, bf16[256,128]{1,0:T(8,128)(2,1)} %param.9, bf16[256,128]{1,0:T(8,128)(2,1)} %param.8), kind=kLoop, calls=%fused_computation.2 | loop fusion | flops 786432 | bytes 524288 | tf_op jit(solution)/shard_map/concatenate | solution.py:347
  14.4 2.0 %collective-permute-done.3.refs_1_ = s32[64,128]{1,0:T(8,128)S(1)} collective-permute-done((s32[64,128]{1,0:T(8,128)S(1)}, s32[64,128]{1,0:T(8,128)S(1)}, u32[]{:S(2)}, u32[]{:S(2)}) %collective-permute-start.3) | collective-permute-done | bytes 32800 | tf_op jit(solution)/shard_map/ppermute | solution.py:345
  17.4 1.6 %collective-permute-start.5 = (bf16[2048,128]{1,0:T(8,128)(2,1)S(1)}, bf16[2048,128]{1,0:T(8,128)(2,1)S(1)}, u32[]{:S(2)}, u32[]{:S(2)}) collective-permute-start(bf16[2048,128]{1,0:T(8,128)(2,1)S(1)} %pad_maximum_fusion.refs_5_), channel_id=1, source_target_pairs={{0,8},{8,16},{16,24},{24,0},{1,9},{9,17},{17,25},{25,1},{2,10},{10... | collective-permute-start | bytes 1572872 | tf_op jit(solution)/shard_map/ppermute | solution.py:349
  19.0 4.0 %collective-permute-start.11 = (bf16[1024,128]{1,0:T(8,128)(2,1)S(1)}, bf16[1024,128]{1,0:T(8,128)(2,1)S(1)}, u32[]{:S(2)}, u32[]{:S(2)}) collective-permute-start(bf16[1024,128]{1,0:T(8,128)(2,1)S(1)} %pad_maximum_fusion.2.refs_1_), channel_id=1, source_target_pairs={{0,3},{1,0},{2,1},{3,2},{4,7},{5,4},{6,5},{7,6},{8,11},{9,8},{10,9... | collective-permute-start | bytes 786440 | tf_op jit(solution)/shard_map/ppermute | solution.py:356
  23.0 5.4 %collective-permute-done.7.refs_6_ = bf16[2048,128]{1,0:T(8,128)(2,1)S(1)} collective-permute-done((bf16[2048,128]{1,0:T(8,128)(2,1)S(1)}, bf16[2048,128]{1,0:T(8,128)(2,1)S(1)}, u32[]{:S(2)}, u32[]{:S(2)}) %collective-permute-start.7) | collective-permute-done | bytes 524320 | tf_op jit(solution)/shard_map/ppermute | solution.py:350
  28.5 1.9 %collective-permute-start.9 = (bf16[1024,128]{1,0:T(8,128)(2,1)S(1)}, bf16[1024,128]{1,0:T(8,128)(2,1)S(1)}, u32[]{:S(2)}, u32[]{:S(2)}) collective-permute-start(bf16[1024,128]{1,0:T(8,128)(2,1)S(1)} %pad_maximum_fusion.2.refs_1_), channel_id=1, source_target_pairs={{0,1},{1,2},{2,3},{3,0},{4,5},{5,6},{6,7},{7,4},{8,9},{9,10},{10,1... | collective-permute-start | bytes 786440 | tf_op jit(solution)/shard_map/ppermute | solution.py:356
  30.5 0.9 %collective-permute-done.5.refs_5_ = bf16[2048,128]{1,0:T(8,128)(2,1)S(1)} collective-permute-done((bf16[2048,128]{1,0:T(8,128)(2,1)S(1)}, bf16[2048,128]{1,0:T(8,128)(2,1)S(1)}, u32[]{:S(2)}, u32[]{:S(2)}) %collective-permute-start.5) | collective-permute-done | bytes 524320 | tf_op jit(solution)/shard_map/ppermute | solution.py:349
  31.4 2.4 %collective-permute-start.8 = (bf16[1024,128]{1,0:T(8,128)(2,1)S(1)}, bf16[1024,128]{1,0:T(8,128)(2,1)S(1)}, u32[]{:S(2)}, u32[]{:S(2)}) collective-permute-start(bf16[1024,128]{1,0:T(8,128)(2,1)S(1)} %slice.9), channel_id=1, source_target_pairs={{0,24},{8,0},{16,8},{24,16},{1,25},{9,1},{17,9},{25,17},{2,26},{10... | collective-permute-start | bytes 786440 | tf_op jit(solution)/shard_map/ppermute | solution.py:352
  33.8 1.1 %collective-permute-done.11.refs_4_ = bf16[1024,128]{1,0:T(8,128)(2,1)S(1)} collective-permute-done((bf16[1024,128]{1,0:T(8,128)(2,1)S(1)}, bf16[1024,128]{1,0:T(8,128)(2,1)S(1)}, u32[]{:S(2)}, u32[]{:S(2)}) %collective-permute-start.11) | collective-permute-done | bytes 262176 | tf_op jit(solution)/shard_map/ppermute | solution.py:356
  34.9 3.7 %collective-permute-done.9.refs_2_ = bf16[1024,128]{1,0:T(8,128)(2,1)S(1)} collective-permute-done((bf16[1024,128]{1,0:T(8,128)(2,1)S(1)}, bf16[1024,128]{1,0:T(8,128)(2,1)S(1)}, u32[]{:S(2)}, u32[]{:S(2)}) %collective-permute-start.9) | collective-permute-done | bytes 262176 | tf_op jit(solution)/shard_map/ppermute | solution.py:356
  38.6 6.5 %near.1 = (bf16[16,256,256]{2,1,0:T(8,128)(2,1)S(1)}, f32[16,280,128]{2,1,0:T(8,128)S(1)}) custom-call(s32[5]{0:T(128)S(1)} %stack.23.me_ref, s32[64,128]{1,0:T(8,128)S(1)} %add_add_fusion.refs_0_, bf16[1024,128]{1,0:T(8,128)(2,1)S(1)} %pad_maximum_fusion.2.refs_1_, bf16[1024,128]{1,0:T(8,128)(2,1)S(1)} %collective-permute-done.9.refs_2_, ...), custom_call_target="tpu_custom_call" | custom-call | flops 3840000000 | bytes 4194304 | tf_op jit(solution)/shard_map/near/pallas_call | solution.py:320
  45.9 0.9 %collective-permute-done.15.refs_11_ = bf16[1024,128]{1,0:T(8,128)(2,1)S(1)} collective-permute-done((bf16[1024,128]{1,0:T(8,128)(2,1)S(1)}, bf16[1024,128]{1,0:T(8,128)(2,1)S(1)}, u32[]{:S(2)}, u32[]{:S(2)}) %collective-permute-start.15) | collective-permute-done | bytes 262176 | tf_op jit(solution)/shard_map/ppermute | solution.py:366
  47.2 11.2 %away.1 = (bf16[1088,128]{1,0:T(8,128)(2,1)S(1)}, bf16[1088,128]{1,0:T(8,128)(2,1)S(1)}, bf16[1088,128]{1,0:T(8,128)(2,1)S(1)}, bf16[3072,256]{1,0:T(8,128)(2,1)S(1)}, bf16[24,256,128]{2,1,0:T(8,128)(2,1)S(1)}) custom-call(s32[5]{0:T(128)S(1)} %stack.23.me_ref, s32[64,128]{1,0:T(8,128)S(1)} %collective-permute-done.2.refs_0_, ...), custom_call_target="tpu_custom_call" | custom-call | flops 8640000000 | bytes 4194304 | tf_op jit(solution)/shard_map/away/pallas_call | solution.py:320
  58.5 3.3 %collective-permute-start.18 = (bf16[1088,128]{1,0:T(8,128)(2,1)S(1)}, bf16[1088,128]{1,0:T(8,128)(2,1)S(1)}, u32[]{:S(2)}, u32[]{:S(2)}) collective-permute-start(bf16[1088,128]{1,0:T(8,128)(2,1)S(1)} %get-tuple-element.43), channel_id=1, source_target_pairs={{0,3},{1,0},{2,1},{3,2},{4,7},{5,4},{6,5},{7,6},{8,11},{9,8},{10,9... | collective-permute-start | bytes 835592 | tf_op jit(solution)/shard_map/ppermute | solution.py:371
  62.7 3.4 %home.1.refs_0_ = bf16[1088,128]{1,0:T(8,128)(2,1)S(1)} custom-call(s32[5]{0:T(128)S(1)} %stack.23.me_ref, s32[64,128]{1,0:T(8,128)S(1)} %collective-permute-done.2.refs_0_, s32[64,128]{1,0:T(8,128)S(1)} %collective-permute-done.3.refs_1_, s32[64,128]{1,0:T(8,128)S(1)} %collective-permute-done.4.refs_2_, ...), custom_call_target="tpu_custom_call" | custom-call | flops 2880000000 | bytes 4194304 | tf_op jit(solution)/shard_map/home/pallas_call | solution.py:320
  66.1 3.0 %collective-permute-done.17.refs_1_ = bf16[1088,128]{1,0:T(8,128)(2,1)S(1)} collective-permute-done((bf16[1088,128]{1,0:T(8,128)(2,1)S(1)}, bf16[1088,128]{1,0:T(8,128)(2,1)S(1)}, u32[]{:S(2)}, u32[]{:S(2)}) %collective-permute-start.17) | collective-permute-done | bytes 278560 | tf_op jit(solution)/shard_map/ppermute | solution.py:371
  69.1 2.9 %collective-permute-done.18.refs_2_ = bf16[1088,128]{1,0:T(8,128)(2,1)S(1)} collective-permute-done((bf16[1088,128]{1,0:T(8,128)(2,1)S(1)}, bf16[1088,128]{1,0:T(8,128)(2,1)S(1)}, u32[]{:S(2)}, u32[]{:S(2)}) %collective-permute-start.18) | collective-permute-done | bytes 278560 | tf_op jit(solution)/shard_map/ppermute | solution.py:371
  72.8 5.1 %collective-permute-start.20 = (bf16[544,128]{1,0:T(8,128)(2,1)S(1)}, bf16[544,128]{1,0:T(8,128)(2,1)S(1)}, u32[]{:S(2)}, u32[]{:S(2)}) collective-permute-start(bf16[544,128]{1,0:T(8,128)(2,1)S(1)} %beyond.1), channel_id=1, source_target_pairs={{0,4},{4,0},{1,5},{5,1},{2,6},{6,2},{3,7},{7,3},{8,12},{12,8},{9,1... | collective-permute-start | bytes 417800 | tf_op jit(solution)/shard_map/ppermute | solution.py:373
  78.1 3.6 %collective-permute-done.20.part = bf16[544,128]{1,0:T(8,128)(2,1)S(1)} collective-permute-done((bf16[544,128]{1,0:T(8,128)(2,1)S(1)}, bf16[544,128]{1,0:T(8,128)(2,1)S(1)}, u32[]{:S(2)}, u32[]{:S(2)}) %collective-permute-start.20) | collective-permute-done | bytes 139296 | tf_op jit(solution)/shard_map/ppermute | solution.py:373
  (36 shorter events, 9.0 us)
Async XLA Ops:
  1.5 11.2 %collective-permute-start.1 = (bf16[512,128]{1,0:T(8,128)(2,1)S(1)}, bf16[512,128]{1,0:T(8,128)(2,1)S(1)}, u32[]{:S(2)}, u32[]{:S(2)}) collective-permute-start(bf16[512,128]{1,0:T(8,128)(2,1)S(1)} %pad_maximum_fusion.3), channel_id=1, source_target_pairs={{0,4},{4,0},{1,5},{5,1},{2,6},{6,2},{3,7},{7,3},{8,12},{12,8},{9,1... | collective-permute-start | bytes 393224 | tf_op jit(solution)/shard_map/ppermute | solution.py:343
  5.8 8.6 %collective-permute-start = (bf16[1024,128]{1,0:T(8,128)(2,1)S(1)}, bf16[1024,128]{1,0:T(8,128)(2,1)S(1)}, u32[]{:S(2)}, u32[]{:S(2)}) collective-permute-start(bf16[1024,128]{1,0:T(8,128)(2,1)S(1)} %pad_maximum_fusion.1), channel_id=1, source_target_pairs={{0,64},{64,0},{1,65},{65,1},{2,66},{66,2},{3,67},{67,3},{4,68},{68... | collective-permute-start | bytes 786440 | tf_op jit(solution)/shard_map/ppermute | solution.py:341
  8.3 6.2 %collective-permute-start.4 = (s32[64,128]{1,0:T(8,128)S(1)}, s32[64,128]{1,0:T(8,128)S(1)}, u32[]{:S(2)}, u32[]{:S(2)}) collective-permute-start(s32[64,128]{1,0:T(8,128)S(1)} %add_add_fusion.refs_0_), channel_id=1, source_target_pairs={{0,24},{8,0},{16,8},{24,16},{1,25},{9,1},{17,9},{25,17},{2,26},{10... | collective-permute-start | bytes 98312 | tf_op jit(solution)/shard_map/ppermute | solution.py:345
  11.0 5.4 %collective-permute-start.3 = (s32[64,128]{1,0:T(8,128)S(1)}, s32[64,128]{1,0:T(8,128)S(1)}, u32[]{:S(2)}, u32[]{:S(2)}) collective-permute-start(s32[64,128]{1,0:T(8,128)S(1)} %add_add_fusion.refs_0_), channel_id=1, source_target_pairs={{0,16},{8,24},{16,0},{24,8},{1,17},{9,25},{17,1},{25,9},{2,18},{10... | collective-permute-start | bytes 98312 | tf_op jit(solution)/shard_map/ppermute | solution.py:345
  11.8 5.1 %collective-permute-start.2 = (s32[64,128]{1,0:T(8,128)S(1)}, s32[64,128]{1,0:T(8,128)S(1)}, u32[]{:S(2)}, u32[]{:S(2)}) collective-permute-start(s32[64,128]{1,0:T(8,128)S(1)} %add_add_fusion.refs_0_), channel_id=1, source_target_pairs={{0,8},{8,16},{16,24},{24,0},{1,9},{9,17},{17,25},{25,1},{2,10},{10... | collective-permute-start | bytes 98312 | tf_op jit(solution)/shard_map/ppermute | solution.py:345
  17.0 11.5 %collective-permute-start.7 = (bf16[2048,128]{1,0:T(8,128)(2,1)S(1)}, bf16[2048,128]{1,0:T(8,128)(2,1)S(1)}, u32[]{:S(2)}, u32[]{:S(2)}) collective-permute-start(bf16[2048,128]{1,0:T(8,128)(2,1)S(1)} %pad_maximum_fusion.refs_5_), channel_id=1, source_target_pairs={{0,24},{8,0},{16,8},{24,16},{1,25},{9,1},{17,9},{25,17},{2,26},{10... | collective-permute-start | bytes 1572872 | tf_op jit(solution)/shard_map/ppermute | solution.py:350
  17.4 14.0 %collective-permute-start.5 = (bf16[2048,128]{1,0:T(8,128)(2,1)S(1)}, bf16[2048,128]{1,0:T(8,128)(2,1)S(1)}, u32[]{:S(2)}, u32[]{:S(2)}) collective-permute-start(bf16[2048,128]{1,0:T(8,128)(2,1)S(1)} %pad_maximum_fusion.refs_5_), channel_id=1, source_target_pairs={{0,8},{8,16},{16,24},{24,0},{1,9},{9,17},{17,25},{25,1},{2,10},{10... | collective-permute-start | bytes 1572872 | tf_op jit(solution)/shard_map/ppermute | solution.py:349
  19.0 19.6 %collective-permute-start.12 = (bf16[2048,128]{1,0:T(8,128)(2,1)S(1)}, bf16[2048,128]{1,0:T(8,128)(2,1)S(1)}, u32[]{:S(2)}, u32[]{:S(2)}) collective-permute-start(bf16[2048,128]{1,0:T(8,128)(2,1)S(1)} %pad_maximum_fusion.refs_5_), channel_id=1, source_target_pairs={{0,32},{32,0},{1,33},{33,1},{2,34},{34,2},{3,35},{35,3},{4,36},{36... | collective-permute-start | bytes 1572872 | tf_op jit(solution)/shard_map/ppermute | solution.py:354
  19.0 15.9 %collective-permute-start.11 = (bf16[1024,128]{1,0:T(8,128)(2,1)S(1)}, bf16[1024,128]{1,0:T(8,128)(2,1)S(1)}, u32[]{:S(2)}, u32[]{:S(2)}) collective-permute-start(bf16[1024,128]{1,0:T(8,128)(2,1)S(1)} %pad_maximum_fusion.2.refs_1_), channel_id=1, source_target_pairs={{0,3},{1,0},{2,1},{3,2},{4,7},{5,4},{6,5},{7,6},{8,11},{9,8},{10,9... | collective-permute-start | bytes 786440 | tf_op jit(solution)/shard_map/ppermute | solution.py:356
  23.0 11.9 %collective-permute-start.10 = (bf16[1024,128]{1,0:T(8,128)(2,1)S(1)}, bf16[1024,128]{1,0:T(8,128)(2,1)S(1)}, u32[]{:S(2)}, u32[]{:S(2)}) collective-permute-start(bf16[1024,128]{1,0:T(8,128)(2,1)S(1)} %pad_maximum_fusion.2.refs_1_), channel_id=1, source_target_pairs={{0,2},{1,3},{2,0},{3,1},{4,6},{5,7},{6,4},{7,5},{8,10},{9,11},{10,... | collective-permute-start | bytes 786440 | tf_op jit(solution)/shard_map/ppermute | solution.py:356
  28.5 10.1 %collective-permute-start.9 = (bf16[1024,128]{1,0:T(8,128)(2,1)S(1)}, bf16[1024,128]{1,0:T(8,128)(2,1)S(1)}, u32[]{:S(2)}, u32[]{:S(2)}) collective-permute-start(bf16[1024,128]{1,0:T(8,128)(2,1)S(1)} %pad_maximum_fusion.2.refs_1_), channel_id=1, source_target_pairs={{0,1},{1,2},{2,3},{3,0},{4,5},{5,6},{6,7},{7,4},{8,9},{9,10},{10,1... | collective-permute-start | bytes 786440 | tf_op jit(solution)/shard_map/ppermute | solution.py:356
  31.4 13.7 %collective-permute-start.8 = (bf16[1024,128]{1,0:T(8,128)(2,1)S(1)}, bf16[1024,128]{1,0:T(8,128)(2,1)S(1)}, u32[]{:S(2)}, u32[]{:S(2)}) collective-permute-start(bf16[1024,128]{1,0:T(8,128)(2,1)S(1)} %slice.9), channel_id=1, source_target_pairs={{0,24},{8,0},{16,8},{24,16},{1,25},{9,1},{17,9},{25,17},{2,26},{10... | collective-permute-start | bytes 786440 | tf_op jit(solution)/shard_map/ppermute | solution.py:352
  34.9 10.2 %collective-permute-start.6 = (bf16[1024,128]{1,0:T(8,128)(2,1)S(1)}, bf16[1024,128]{1,0:T(8,128)(2,1)S(1)}, u32[]{:S(2)}, u32[]{:S(2)}) collective-permute-start(bf16[1024,128]{1,0:T(8,128)(2,1)S(1)} %slice.8), channel_id=1, source_target_pairs={{0,8},{8,16},{16,24},{24,0},{1,9},{9,17},{17,25},{25,1},{2,10},{10... | collective-permute-start | bytes 786440 | tf_op jit(solution)/shard_map/ppermute | solution.py:351
  34.9 11.1 %collective-permute-start.14 = (bf16[2048,128]{1,0:T(8,128)(2,1)S(1)}, bf16[2048,128]{1,0:T(8,128)(2,1)S(1)}, u32[]{:S(2)}, u32[]{:S(2)}) collective-permute-start(bf16[2048,128]{1,0:T(8,128)(2,1)S(1)} %collective-permute-done.7.refs_6_), channel_id=1, source_target_pairs={{0,32},{32,0},{1,33},{33,1},{2,34},{34,2},{3,35},{35,3},{4,36},{36... | collective-permute-start | bytes 1572872 | tf_op jit(solution)/shard_map/ppermute | solution.py:354
  38.6 7.4 %collective-permute-start.13 = (bf16[2048,128]{1,0:T(8,128)(2,1)S(1)}, bf16[2048,128]{1,0:T(8,128)(2,1)S(1)}, u32[]{:S(2)}, u32[]{:S(2)}) collective-permute-start(bf16[2048,128]{1,0:T(8,128)(2,1)S(1)} %collective-permute-done.5.refs_5_), channel_id=1, source_target_pairs={{0,32},{32,0},{1,33},{33,1},{2,34},{34,2},{3,35},{35,3},{4,36},{36... | collective-permute-start | bytes 1572872 | tf_op jit(solution)/shard_map/ppermute | solution.py:354
  45.1 1.7 %collective-permute-start.15 = (bf16[1024,128]{1,0:T(8,128)(2,1)S(1)}, bf16[1024,128]{1,0:T(8,128)(2,1)S(1)}, u32[]{:S(2)}, u32[]{:S(2)}) collective-permute-start(bf16[1024,128]{1,0:T(8,128)(2,1)S(1)} %collective-permute-done.6.refs_7_), channel_id=1, source_target_pairs={{0,32},{32,0},{1,33},{33,1},{2,34},{34,2},{3,35},{35,3},{4,36},{36... | collective-permute-start | bytes 786440 | tf_op jit(solution)/shard_map/ppermute | solution.py:366
  45.7 1.5 %collective-permute-start.16 = (bf16[1024,128]{1,0:T(8,128)(2,1)S(1)}, bf16[1024,128]{1,0:T(8,128)(2,1)S(1)}, u32[]{:S(2)}, u32[]{:S(2)}) collective-permute-start(bf16[1024,128]{1,0:T(8,128)(2,1)S(1)} %collective-permute-done.8.refs_8_), channel_id=1, source_target_pairs={{0,32},{32,0},{1,33},{33,1},{2,34},{34,2},{3,35},{35,3},{4,36},{36... | collective-permute-start | bytes 786440 | tf_op jit(solution)/shard_map/ppermute | solution.py:366
  58.4 10.7 %collective-permute-start.17 = (bf16[1088,128]{1,0:T(8,128)(2,1)S(1)}, bf16[1088,128]{1,0:T(8,128)(2,1)S(1)}, u32[]{:S(2)}, u32[]{:S(2)}) collective-permute-start(bf16[1088,128]{1,0:T(8,128)(2,1)S(1)} %get-tuple-element.42), channel_id=1, source_target_pairs={{0,2},{1,3},{2,0},{3,1},{4,6},{5,7},{6,4},{7,5},{8,10},{9,11},{10,... | collective-permute-start | bytes 835592 | tf_op jit(solution)/shard_map/ppermute | solution.py:371
  58.5 13.5 %collective-permute-start.18 = (bf16[1088,128]{1,0:T(8,128)(2,1)S(1)}, bf16[1088,128]{1,0:T(8,128)(2,1)S(1)}, u32[]{:S(2)}, u32[]{:S(2)}) collective-permute-start(bf16[1088,128]{1,0:T(8,128)(2,1)S(1)} %get-tuple-element.43), channel_id=1, source_target_pairs={{0,3},{1,0},{2,1},{3,2},{4,7},{5,4},{6,5},{7,6},{8,11},{9,8},{10,9... | collective-permute-start | bytes 835592 | tf_op jit(solution)/shard_map/ppermute | solution.py:371
  61.9 10.7 %collective-permute-start.19 = (bf16[1088,128]{1,0:T(8,128)(2,1)S(1)}, bf16[1088,128]{1,0:T(8,128)(2,1)S(1)}, u32[]{:S(2)}, u32[]{:S(2)}) collective-permute-start(bf16[1088,128]{1,0:T(8,128)(2,1)S(1)} %get-tuple-element.44), channel_id=1, source_target_pairs={{0,1},{1,2},{2,3},{3,0},{4,5},{5,6},{6,7},{7,4},{8,9},{9,10},{10,1... | collective-permute-start | bytes 835592 | tf_op jit(solution)/shard_map/ppermute | solution.py:371
  72.8 9.0 %collective-permute-start.20 = (bf16[544,128]{1,0:T(8,128)(2,1)S(1)}, bf16[544,128]{1,0:T(8,128)(2,1)S(1)}, u32[]{:S(2)}, u32[]{:S(2)}) collective-permute-start(bf16[544,128]{1,0:T(8,128)(2,1)S(1)} %beyond.1), channel_id=1, source_target_pairs={{0,4},{4,0},{1,5},{5,1},{2,6},{6,2},{3,7},{7,3},{8,12},{12,8},{9,1... | collective-permute-start | bytes 417800 | tf_op jit(solution)/shard_map/ppermute | solution.py:373
